TPU v7x, 512 devices: a whole 4x4x16 slice. The times are simulated.
512 devices in a mesh: inner: 16 (over z_hi, x, core), outer: 32 (over y, z_lo).
Axes of the slice: x: 4, y: 4, z: 16 (z_hi: 2, z_lo: 8; z = z_hi * 8 + z_lo), core: 2. Of those that a mesh axis runs over, the one named last changes fastest.
Arguments:
- queries: bfloat16 [65536, 1024], P(('inner', 'outer')), may hold values from -6 to 6
- keys: bfloat16 [65536, 128], P(('inner', 'outer')), may hold values from -6 to 6
- values: bfloat16 [65536, 128], P(('inner', 'outer')), may hold values from -6 to 6
- lengths: int32 [16], replicated, may hold values from 1 to 16384, 65536 in all
Outputs:
- attended: bfloat16 [65536, 1024], P(('inner', 'outer'))
Inputs may be any that keep to these rules, and one draw needn't show every extreme that they name: lengths sum to 65536; the longest is exactly 16384.
All inputs are finite; a program needn't handle non-finite values.
Results may differ from a plain program's by a relative error of at most 0.0085.
Values may be sent and summed in bfloat16 or wider, within the bound.
No kernel may reach another device: no remote copies, remote signals or barrier semaphores. Data moves between devices by JAX's collectives and lax.ppermute only.
A program may use at most 64 MiB of HBM per device.

v0:
```python
import functools
import math

import jax
import jax.numpy as jnp
from jax import lax
from jax.experimental import pallas as pl
from jax.experimental.pallas import tpu as pltpu
from jax.sharding import PartitionSpec as P

AXES = ("inner", "outer")
HEAD = 128
HEADS = 8
TOKENS = 128
DOCS = 16
ROWS = HEADS * TOKENS
SPAN = 16384
SCALE = HEAD**-0.5 * math.log2(math.e)
ROOM = 50.0
LARGEST_KEY = 6.0
HEADROOM = 100.0
LOWEST = -float(2**66)
MASKED = -1e30
STATS = 16


def coords(i):
    inner, outer = divmod(i, 32)
    return dict(zh=inner // 8, u=inner // 4 % 2, xp=inner // 2 % 2, c=inner % 2, y=outer // 8, w=outer // 2 % 4, zp=outer % 2)


def index(d):
    inner = d["zh"] * 8 + d["u"] * 4 + d["xp"] * 2 + d["c"]
    return inner * 32 + d["y"] * 8 + d["w"] * 2 + d["zp"]


def move(x, f):
    pairs = []
    for i in range(512):
        d = coords(i)
        to = f(**d)
        if to is not None:
            pairs.append((i, index({**d, **to})))
    return lax.ppermute(x, AXES, pairs)


def to_next_span(zh, u, xp, y, w, **_):
    span = 2 * zh + u + 1
    if span > 3:
        return None
    return dict(zh=span // 2, u=span % 2, xp=xp ^ (y & 1), w=3 - w if span == 2 else w)


def halves(x):
    high = x.astype(jnp.bfloat16).astype(jnp.float32)
    return high, (x - high).astype(jnp.bfloat16).astype(jnp.float32)


def stacked(row, *rows):
    out = jnp.zeros(row.shape, jnp.float32)
    for i, x in enumerate(rows):
        out = jnp.where(row == i, x, out)
    return out.astype(jnp.bfloat16)


def prep_kernel(q_ref, k_ref, o_ref):
    key_t = k_ref[...].T.astype(jnp.float32)
    row = lax.broadcasted_iota(jnp.int32, (STATS, TOKENS), 0)
    for h in range(HEADS):
        s = slice(h * HEAD, (h + 1) * HEAD)
        query_t = q_ref[:, s].T
        o_ref[:HEAD, s] = query_t
        query = query_t.astype(jnp.float32)
        shift = jnp.sum(query * key_t, axis=0, keepdims=True) * SCALE + ROOM
        high, low = halves(shift)
        highest = jnp.sum(jnp.abs(query), axis=0, keepdims=True) * (LARGEST_KEY * SCALE)
        unsafe = jnp.where(highest - shift > HEADROOM, 1.0, 0.0)
        o_ref[HEAD:, s] = stacked(row, high, low, unsafe)


def pair_kernel(a_ref, b_ref, out_ref):
    for i, ref in enumerate((a_ref, b_ref)):
        out_ref[0, i, 0] = ref[0]
        out_ref[0, i, 1] = ref[1].T


def join_kernel(*refs):
    *in_refs, out_ref = refs
    at = 0
    for ref in in_refs:
        out_ref[at : at + ref.shape[0]] = ref[...]
        at += ref.shape[0]


def near(y, cc):
    return jnp.where(cc == 0, y ^ 1, 3 - y)


def place_of(cd):
    me = cd[0]
    return me >> 7, (me >> 6) & 1, (me >> 5) & 1, (me >> 3) & 3, (me >> 1) & 3, me & 1


def place(cd, flip, kind, src, slot):
    span, xp, c, y, w, zp = place_of(cd)
    cc = c ^ flip
    yy = {"own": y, "one": near(y, cc), "two": near(y, 1 - cc), "far": (y + 2) & 3}[kind]
    ww = w ^ jnp.where(cc == 0, (0, 2, 1, 3)[slot], slot)
    ww = jnp.where((src == 1) & (span == 2), 3 - ww, ww)
    return SPAN * (span - src) + 8192 * (xp ^ (yy & 1)) + 4096 * cc + 1024 * yy + 256 * ww + 128 * zp


def first_of(cd, qi):
    span, xp, c, y, w, zp = place_of(cd)
    return SPAN * span + 8192 * (xp ^ (qi >> 1)) + 4096 * c + 1024 * y + 256 * w + 128 * (zp ^ (qi & 1))


def start_of(lengths, positions):
    end, start = jnp.int32(0), jnp.zeros_like(positions)
    for d in range(DOCS):
        end = end + lengths[d]
        start = jnp.where(end <= positions, end, start)
    return start


def per_head(allowed, x, other):
    return jnp.concatenate(
        [jnp.where(allowed, x[:, h * TOKENS : (h + 1) * TOKENS], other) for h in range(HEADS)], axis=1
    )


def fold(cd, lengths, info, tiles, qi, qt_ref, at, m_ref, l_ref, acc_ref):
    q_first, start_first, start_last, unsafe = (info[4 * qi + j] for j in range(4))
    safe = unsafe == 0

    def visit(src, blocks, places, masked, online):
        key = jnp.concatenate([ref[j, src, 0] for ref, j in blocks], axis=0)
        value_t = jnp.concatenate([ref[j, src, 1] for ref, j in blocks], axis=1)
        if masked:
            iota = lax.broadcasted_iota(jnp.int32, (TOKENS, TOKENS), 0)
            key_pos = jnp.concatenate([iota + p for p in places], axis=0)
            query_pos = q_first + lax.broadcasted_iota(jnp.int32, (1, TOKENS), 1)
            allowed = (key_pos <= query_pos) & (key_pos >= start_of(lengths, query_pos))
        scores = lax.dot(key, qt_ref[qi, :HEAD], preferred_element_type=jnp.float32)
        if not online:
            weights = jnp.exp2(scores * SCALE - m_ref[at])
            if masked:
                weights = per_head(allowed, weights, 0.0)
            row = lax.broadcasted_iota(jnp.int32, (STATS, value_t.shape[1]), 0)
            ones = jnp.where(row == 0, 1.0, 0.0).astype(jnp.bfloat16)
            value_t = jnp.concatenate([value_t, ones], axis=0)
            summed = lax.dot(value_t, weights.astype(jnp.bfloat16), preferred_element_type=jnp.float32)
            acc_ref[at] += summed[:HEAD]
            l_ref[at] += summed[HEAD : HEAD + 1]
            return
        scores = per_head(allowed, scores, MASKED)
        old = m_ref[at]
        new = jnp.maximum(old, jnp.max(scores, axis=0, keepdims=True) * SCALE)
        weights = jnp.exp2(scores * SCALE - new)
        factor = jnp.exp2(old - new)
        m_ref[at] = new
        l_ref[at] = l_ref[at] * factor + jnp.sum(weights, axis=0, keepdims=True)
        acc_ref[at] = acc_ref[at] * factor + lax.dot(
            value_t, weights.astype(jnp.bfloat16), preferred_element_type=jnp.float32
        )

    def one(src, carry):
        found = []
        for flip, kind, blocks in tiles:
            places = [place(cd, flip, kind, src, j) for j in range(4)]
            low = functools.reduce(jnp.minimum, places)
            high = functools.reduce(jnp.maximum, places) + (TOKENS - 1)
            active = (high >= start_first) & (low <= q_first + (TOKENS - 1))
            whole = active & (high <= q_first) & (low >= start_last) & safe
            found.append((blocks, places, active, whole))
        together = False
        if len(found) == 2:
            together = found[0][3] & found[1][3]

            @pl.when(together)
            def _():
                visit(src, found[0][0] + found[1][0], None, False, False)

        for blocks, places, active, whole in found:

            @pl.when(whole & jnp.logical_not(together))
            def _(blocks=blocks, places=places):
                visit(src, blocks, places, False, False)

            @pl.when(active & jnp.logical_not(whole) & safe)
            def _(blocks=blocks, places=places):
                visit(src, blocks, places, True, False)

            @pl.when(active & jnp.logical_not(safe))
            def _(blocks=blocks, places=places):
                visit(src, blocks, places, True, True)

        return carry

    lax.fori_loop(0, 2, one, 0)


def tiles_of(kinds, refs):
    out, at = [], 0
    for flip, names, shared in kinds:
        each = 4 // shared
        for i, name in enumerate(names):
            out.append((flip, name, [(refs[at + k], each * i + j) for k in range(shared) for j in range(each)]))
        at += shared
    return out


def own_kernel(kinds, n, cd, lengths, *refs):
    tiles, rest = tiles_of(kinds, refs), refs[n:]
    a_ref, b_ref, c_ref, info, qt_ref, m_ref, l_ref, acc_ref = rest
    qt_ref[0] = a_ref[...]
    qt_ref[1] = b_ref[...]
    qt_ref[2:] = c_ref[...]

    def one(qi, carry):
        rows = qt_ref[qi, HEAD:].astype(jnp.float32)
        unsafe = (jnp.max(rows[2:3]) > 0.5).astype(jnp.int32)
        q_first = first_of(cd, qi)
        info[4 * qi] = q_first
        info[4 * qi + 1] = start_of(lengths, q_first)
        info[4 * qi + 2] = start_of(lengths, q_first + (TOKENS - 1))
        info[4 * qi + 3] = unsafe
        m_ref[qi] = jnp.where(unsafe == 0, rows[0:1] + rows[1:2], LOWEST)
        l_ref[qi] = jnp.zeros_like(l_ref[qi])
        acc_ref[qi] = jnp.zeros_like(acc_ref[qi])
        fold(cd, lengths, info, tiles, qi, qt_ref, qi, m_ref, l_ref, acc_ref)
        return carry

    lax.fori_loop(0, 4, one, 0)


def part_kernel(kinds, n, cd, lengths, info, *refs):
    tiles, (qt_ref, *state, m_ref, l_ref, acc_ref) = tiles_of(kinds, refs), refs[n:]

    def one(qi, carry):
        m_ref[qi], l_ref[qi], acc_ref[qi] = (r[qi] for r in state)
        fold(cd, lengths, info, tiles, qi, qt_ref, qi, m_ref, l_ref, acc_ref)
        return carry

    lax.fori_loop(0, 4, one, 0)


def last_kernel(kinds, n, qis, cd, lengths, info, *refs):
    tiles, (qt_ref, *state) = tiles_of(kinds, refs), refs[n : n + 4]
    *out_refs, m_ref, l_ref, acc_ref = refs[n + 4 :]
    for qi, out_ref in zip(qis, out_refs):
        m_ref[0], l_ref[0], acc_ref[0] = (r[qi] for r in state)
        fold(cd, lengths, info, tiles, qi, qt_ref, 0, m_ref, l_ref, acc_ref)
        high, low = halves(m_ref[0])
        factor = jnp.exp2(m_ref[0] - (high + low))
        out_ref[:HEAD] = (acc_ref[0] * factor).astype(jnp.bfloat16)
        row = lax.broadcasted_iota(jnp.int32, (STATS, ROWS), 0)
        out_ref[HEAD:] = stacked(row, high, low, *halves(l_ref[0] * factor))


def unpacked(ref):
    stats = ref[HEAD:].astype(jnp.float32)
    return stats[0:1] + stats[1:2], stats[2:3] + stats[3:4], ref[:HEAD]


def final_kernel(kinds, n, cd, lengths, info, *refs):
    tiles, (qt_ref, packed_ref, *state) = tiles_of(kinds, refs), refs[n : n + 5]
    m_ref, l_ref, acc_ref = refs[n + 5 :]
    m_ref[0], l_ref[0], acc_ref[0] = (r[0] for r in state)
    fold(cd, lengths, info, tiles, 0, qt_ref, 0, m_ref, l_ref, acc_ref)
    m_a, l_a, acc_a = unpacked(packed_ref)
    m_b = m_ref[0]
    top = jnp.maximum(m_a, m_b)
    f_a, f_b = jnp.exp2(m_a - top), jnp.exp2(m_b - top)
    m_ref[0] = top
    l_ref[0] = l_a * f_a + l_ref[0] * f_b
    acc_ref[0] = acc_a.astype(jnp.float32) * f_a + acc_ref[0] * f_b


def combine_kernel(a_ref, b_ref, m_ref, l_ref, acc_ref, out_ref):
    states = [unpacked(a_ref), unpacked(b_ref), (m_ref[0], l_ref[0], acc_ref[0])]
    top = functools.reduce(jnp.maximum, [m for m, _, _ in states])
    factors = [jnp.exp2(m - top) for m, _, _ in states]
    total = sum(f * l for f, (_, l, _) in zip(factors, states))
    inverse = [f / total for f in factors]
    for h in range(HEADS):
        s = slice(h * TOKENS, (h + 1) * TOKENS)
        summed = sum(i[:, s] * acc[:, s].astype(jnp.float32) for i, (_, _, acc) in zip(inverse, states))
        out_ref[:, s] = summed.T.astype(jnp.bfloat16)


VMEM = pl.BlockSpec(memory_space=pltpu.VMEM)
SMEM = pl.BlockSpec(memory_space=pltpu.SMEM)
LONG = 2**13
STATE = [
    jax.ShapeDtypeStruct((4, 1, ROWS), jnp.float32),
    jax.ShapeDtypeStruct((4, 1, ROWS), jnp.float32),
    jax.ShapeDtypeStruct((4, HEAD, ROWS), jnp.float32),
]
PACKED = jax.ShapeDtypeStruct((HEAD + STATS, ROWS), jnp.bfloat16)
SCRATCH = [
    pltpu.VMEM((1, 1, ROWS), jnp.float32),
    pltpu.VMEM((1, 1, ROWS), jnp.float32),
    pltpu.VMEM((1, HEAD, ROWS), jnp.float32),
]


def call(kernel, name, out_shape, scalars, arrays, out_specs, cost=1, scratch=()):
    return pl.pallas_call(
        kernel,
        out_shape=out_shape,
        in_specs=[SMEM] * len(scalars) + [VMEM] * len(arrays),
        out_specs=out_specs,
        scratch_shapes=list(scratch),
        compiler_params=pltpu.CompilerParams(vmem_limit_bytes=16 * 2**20),
        cost_estimate=pl.CostEstimate(
            flops=cost * 2**20, bytes_accessed=cost * 2**10, transcendentals=cost * 2**10
        ),
        name=name,
    )(*scalars, *arrays)


def join(*arrays, cost=1):
    shape = (sum(a.shape[0] for a in arrays), *arrays[0].shape[1:])
    return call(join_kernel, "join", jax.ShapeDtypeStruct(shape, jnp.bfloat16), (), arrays, VMEM, cost)


def shards(queries, keys, values, lengths):
    cd = (lax.axis_index("inner") * 32 + lax.axis_index("outer")).astype(jnp.int32).reshape(1)
    scalars = (cd, lengths)

    def to_slot(s):
        return lambda xp, zp, **_: dict(xp=xp ^ (s // 2), zp=zp ^ (s % 2))

    def swap(x):
        return move(x, lambda c, **_: dict(c=1 - c))

    raw = jnp.stack([keys, values])
    qt = pl.pallas_call(prep_kernel, out_shape=PACKED, in_specs=[VMEM] * 2, out_specs=VMEM, name="prep")(
        queries, keys
    )
    with jax.named_scope("queries_z"):
        qz = move(qt, to_slot(1))

    with jax.named_scope("keys_x"):
        before = move(raw, to_next_span)
        mine = move(raw, lambda xp, y, **_: dict(xp=xp ^ (y & 1)))
    with jax.named_scope("keys_z1"):
        shape = jax.ShapeDtypeStruct((1, 2, 2, TOKENS, HEAD), jnp.bfloat16)
        held = call(pair_kernel, "pair", shape, (), [mine, before], VMEM, LONG)
        got = move(held, lambda w, c, **_: dict(w=w ^ (1 if c else 2)))
    with jax.named_scope("queries_x"):
        qx = move(jnp.stack([qt, qz]), to_slot(2))
    def along_y1(x):
        return move(x, lambda y, c, **_: dict(y=3 - y if c else y ^ 1))

    def along_y2(x):
        return move(x, lambda y, c, **_: dict(y=y ^ 1 if c else 3 - y))

    with jax.named_scope("keys_z2"):
        half = join(held, got)
        rest = move(half, lambda w, c, **_: dict(w=w ^ (2 if c else 1)))
    with jax.named_scope("keys_y1"):
        one_half = along_y1(half)
        held = join(half, rest, cost=LONG)
        rest, held, one_half = lax.optimization_barrier((rest, held, one_half))
        one_rest = along_y1(rest)
    with jax.named_scope("keys_y2"):
        far_half = along_y2(join(half, one_half))

    info, q4, *state = call(
        functools.partial(own_kernel, [(0, ["own"], 1)], 1),
        "own",
        [jax.ShapeDtypeStruct((16,), jnp.int32), jax.ShapeDtypeStruct((4, *PACKED.shape), jnp.bfloat16)] + STATE,
        scalars,
        [held, qt, qz, qx],
        [SMEM] + [VMEM] * 4,
    )
    scalars = (cd, lengths, info)

    def part(name, kinds, arrays, state):
        kernel = functools.partial(part_kernel, kinds, len(arrays))
        return call(kernel, name, STATE, scalars, [*arrays, q4, *state], [VMEM] * 3)

    one_rest, far_half, state = lax.optimization_barrier((one_rest, far_half, state))
    with jax.named_scope("keys_y2"):
        far_rest = along_y2(join(rest, one_rest))
    one = join(one_half, one_rest)
    with jax.named_scope("keys_c1"):
        held_o = swap(held)
        one_o = swap(one)
        far_half_o = swap(far_half)
    state = part("one", [(0, ["one"], 1)], [one], state)
    state = part("other", [(1, ["own"], 1), (1, ["one"], 1)], [held_o, one_o], state)
    far_rest, far_half_o, state = lax.optimization_barrier((far_rest, far_half_o, state))
    with jax.named_scope("keys_c2"):
        far_rest_o = swap(far_rest)
    state = part("far", [(0, ["two", "far"], 2)], [far_half, far_rest], state)
    kinds = [(1, ["two", "far"], 2)]
    far_o = [far_half_o, far_rest_o]
    sent = {}
    for qis in ((3,), (2, 1)):
        kernel = functools.partial(last_kernel, kinds, 2, qis)
        packed = call(
            kernel, "last", [PACKED] * len(qis), scalars, [*far_o, q4, *state], [VMEM] * len(qis), 1, SCRATCH
        )
        packed, state = lax.optimization_barrier((packed, state))
        sent.update(zip(qis, packed))
    with jax.named_scope("sums"):
        got = {s: move(sent[s], to_slot(s)) for s in (3, 2, 1)}
    shape = [jax.ShapeDtypeStruct((1, *x.shape[1:]), x.dtype) for x in STATE]
    kernel = functools.partial(final_kernel, kinds, 2)
    state = call(kernel, "final", shape, scalars, [*far_o, q4, got[3], *state], [VMEM] * 3, LONG)
    out_shape = jax.ShapeDtypeStruct((TOKENS, ROWS), jnp.bfloat16)
    return call(combine_kernel, "combine", out_shape, (), [got[2], got[1], *state], VMEM)


def solution(mesh):
    spec = P(AXES, None)
    return jax.shard_map(shards, mesh=mesh, in_specs=(spec, spec, spec, P()), out_specs=spec, check_vma=False)
```

profile of v0, /device:TPU:4, one launch (start us, length us, event | category | flops | bytes accessed | tf_op | source)
XLA Modules:
  0.0 105.0 jit_solution(430259981900575685)
XLA Ops:
  0.0 0.8 pad_maximum_fusion.1
  0.8 11.8 %collective-permute-start.1 = (bf16[2,128,128]{2,1,0:T(8,128)(2,1)S(1)}, bf16[2,128,128]{2,1,0:T(8,128)(2,1)S(1)}, u32[]{:S(2)}, u32[]{:S(2)}) collective-permute-start(bf16[2,128,128]{2,1,0:T(8,128)(2,1)S(1)} %pad_maximum_fusion.1), channel_id=1, source_target_pairs={{0,128},{1,129},{2,130},{3,131},{4,132},{5,133},{6,134},{7,135},{8... | collective-permute-start | bytes 196616 | tf_op jit(solution)/shard_map/keys_x/ppermute | solution.py:44
  13.2 1.9 %prep.1.refs_1_ = bf16[144,1024]{1,0:T(8,128)(2,1)} custom-call(bf16[128,1024]{1,0:T(8,128)(2,1)} %q_ref.1, bf16[128,128]{1,0:T(8,128)(2,1)} %k_ref.1), custom_call_target="tpu_custom_call" | custom-call | tf_op jit(solution)/shard_map/prep/pallas_call | solution.py:339
  15.1 3.0 %collective-permute-start.5 = (bf16[144,1024]{1,0:T(8,128)(2,1)}, bf16[144,1024]{1,0:T(8,128)(2,1)S(1)}, u32[]{:S(2)}, u32[]{:S(2)}) collective-permute-start(bf16[144,1024]{1,0:T(8,128)(2,1)} %prep.1.refs_1_), channel_id=1, source_target_pairs={{0,1},{1,0},{2,3},{3,2},{4,5},{5,4},{6,7},{7,6},{8,9},{9,8},{10,11... | collective-permute-start | bytes 884744 | tf_op jit(solution)/shard_map/queries_z/ppermute | solution.py:44
  18.3 7.3 %collective-permute-start.2 = (bf16[1,2,2,128,128]{4,3,2,1,0:T(8,128)(2,1)S(1)}, bf16[1,2,2,128,128]{4,3,2,1,0:T(8,128)(2,1)S(1)}, u32[]{:S(2)}, u32[]{:S(2)}) collective-permute-start(bf16[1,2,2,128,128]{4,3,2,1,0:T(8,128)(2,1)S(1)} %pair.1.refs_0_), channel_id=1, source_target_pairs={{0,4},{1,5},{2,6},{3,7},{4,0},{5,1},{6,2},{7,3},{8,12},{9,13},{10,... | collective-permute-start | bytes 393224 | tf_op jit(solution)/shard_map/keys_z1/ppermute | solution.py:44
  25.5 3.6 %collective-permute-done.2.refs_1_ = bf16[1,2,2,128,128]{4,3,2,1,0:T(8,128)(2,1)S(1)} collective-permute-done((bf16[1,2,2,128,128]{4,3,2,1,0:T(8,128)(2,1)S(1)}, bf16[1,2,2,128,128]{4,3,2,1,0:T(8,128)(2,1)S(1)}, u32[]{:S(2)}, u32[]{:S(2)}) %collective-permute-start.2) | collective-permute-done | bytes 131104 | tf_op jit(solution)/shard_map/keys_z1/ppermute | solution.py:44
  29.2 6.9 %collective-permute-start.3 = (bf16[2,2,2,128,128]{4,3,2,1,0:T(8,128)(2,1)S(1)}, bf16[2,2,2,128,128]{4,3,2,1,0:T(8,128)(2,1)S(1)}, u32[]{:S(2)}, u32[]{:S(2)}) collective-permute-start(bf16[2,2,2,128,128]{4,3,2,1,0:T(8,128)(2,1)S(1)} %join.5.refs_0_), channel_id=1, source_target_pairs={{0,2},{1,3},{2,0},{3,1},{4,6},{5,7},{6,4},{7,5},{8,10},{9,11},{10,... | collective-permute-start | bytes 786440 | tf_op jit(solution)/shard_map/keys_z2/ppermute | solution.py:44
  36.0 5.8 %collective-permute-start.4 = (bf16[2,2,2,128,128]{4,3,2,1,0:T(8,128)(2,1)S(1)}, bf16[2,2,2,128,128]{4,3,2,1,0:T(8,128)(2,1)S(1)}, u32[]{:S(2)}, u32[]{:S(2)}) collective-permute-start(bf16[2,2,2,128,128]{4,3,2,1,0:T(8,128)(2,1)S(1)} %join.5.refs_0_), channel_id=1, source_target_pairs={{0,8},{1,9},{2,10},{3,11},{4,12},{5,13},{6,14},{7,15},{8,0},{9,1},... | collective-permute-start | bytes 786440 | tf_op jit(solution)/shard_map/keys_y1/ppermute | solution.py:44
  41.9 0.9 pad_maximum_fusion
  42.8 2.9 %collective-permute-start.6 = (bf16[2,144,1024]{2,1,0:T(8,128)(2,1)}, bf16[2,144,1024]{2,1,0:T(8,128)(2,1)S(1)}, u32[]{:S(2)}, u32[]{:S(2)}) collective-permute-start(bf16[2,144,1024]{2,1,0:T(8,128)(2,1)} %pad_maximum_fusion), channel_id=1, source_target_pairs={{0,64},{1,65},{2,66},{3,67},{4,68},{5,69},{6,70},{7,71},{8,72},{9,... | collective-permute-start | bytes 1769480 | tf_op jit(solution)/shard_map/queries_x/ppermute | solution.py:44
  46.2 5.4 %collective-permute-start.8 = (bf16[4,2,2,128,128]{4,3,2,1,0:T(8,128)(2,1)S(1)}, bf16[4,2,2,128,128]{4,3,2,1,0:T(8,128)(2,1)S(1)}, u32[]{:S(2)}, u32[]{:S(2)}) collective-permute-start(bf16[4,2,2,128,128]{4,3,2,1,0:T(8,128)(2,1)S(1)} %join.7), channel_id=1, source_target_pairs={{0,24},{1,25},{2,26},{3,27},{4,28},{5,29},{6,30},{7,31},{8,16},{9,... | collective-permute-start | bytes 1572872 | tf_op jit(solution)/shard_map/keys_y2/ppermute | solution.py:44
  51.6 1.9 %collective-permute-start.7 = (bf16[2,2,2,128,128]{4,3,2,1,0:T(8,128)(2,1)S(1)}, bf16[2,2,2,128,128]{4,3,2,1,0:T(8,128)(2,1)S(1)}, u32[]{:S(2)}, u32[]{:S(2)}) collective-permute-start(bf16[2,2,2,128,128]{4,3,2,1,0:T(8,128)(2,1)S(1)} %collective-permute-done.3.refs_1_.refs_0_), channel_id=1, source_target_pairs={{0,8},{1,9},{2,10},{3,11},{4,12},{5,13},{6,14},{7,15},{8,0},{9,1},... | collective-permute-start | bytes 786440 | tf_op jit(solution)/shard_map/keys_y1/ppermute | solution.py:44
  53.5 4.2 %collective-permute-start.11 = (bf16[4,2,2,128,128]{4,3,2,1,0:T(8,128)(2,1)S(1)}, bf16[4,2,2,128,128]{4,3,2,1,0:T(8,128)(2,1)S(1)}, u32[]{:S(2)}, u32[]{:S(2)}) collective-permute-start(bf16[4,2,2,128,128]{4,3,2,1,0:T(8,128)(2,1)S(1)} %join.6.refs_0_), channel_id=1, source_target_pairs={{0,32},{1,33},{2,34},{3,35},{4,36},{5,37},{6,38},{7,39},{8,40},{9,... | collective-permute-start | bytes 1572872 | tf_op jit(solution)/shard_map/keys_c1/ppermute | solution.py:44
  57.7 1.2 %collective-permute-done.6.refs_3_ = bf16[2,144,1024]{2,1,0:T(8,128)(2,1)S(1)} collective-permute-done((bf16[2,144,1024]{2,1,0:T(8,128)(2,1)}, bf16[2,144,1024]{2,1,0:T(8,128)(2,1)S(1)}, u32[]{:S(2)}, u32[]{:S(2)}) %collective-permute-start.6) | collective-permute-done | bytes 589856 | tf_op jit(solution)/shard_map/queries_x/ppermute | solution.py:44
  58.9 3.4 %own.1 = (s32[16]{0:T(128)S(1)}, bf16[4,144,1024]{2,1,0:T(8,128)(2,1)S(1)}, f32[4,1,1024]{2,1,0:T(1,128)S(1)}, f32[4,1,1024]{2,1,0:T(1,128)S(1)}, f32[4,128,1024]{2,1,0:T(8,128)S(1)}) custom-call(s32[1]{0:T(128)} %bitcast.cd, s32[16]{0:T(128)S(1)} %copy-done.1, bf16[4,2,2,128,128]{4,3,2,1,0:T(8,128)(2,1)S(1)} %join.6.refs_0_, bf16[144,1024]{1,0:T(8,128)(2,1)S(1)} %copy-done, ...), custom_call_target="tpu_custom_call" | custom-call | flops 1048576 | bytes 1024 | tf_op jit(solution)/shard_map/own/pallas_call | solution.py:309
  62.4 1.9 %collective-permute-start.12 = (bf16[4,2,2,128,128]{4,3,2,1,0:T(8,128)(2,1)S(1)}, bf16[4,2,2,128,128]{4,3,2,1,0:T(8,128)(2,1)S(1)}, u32[]{:S(2)}, u32[]{:S(2)}) collective-permute-start(bf16[4,2,2,128,128]{4,3,2,1,0:T(8,128)(2,1)S(1)} %join.9.refs_0_), channel_id=1, source_target_pairs={{0,32},{1,33},{2,34},{3,35},{4,36},{5,37},{6,38},{7,39},{8,40},{9,... | collective-permute-start | bytes 1572872 | tf_op jit(solution)/shard_map/keys_c1/ppermute | solution.py:44
  64.3 4.5 %collective-permute-start.9 = (bf16[4,2,2,128,128]{4,3,2,1,0:T(8,128)(2,1)S(1)}, bf16[4,2,2,128,128]{4,3,2,1,0:T(8,128)(2,1)S(1)}, u32[]{:S(2)}, u32[]{:S(2)}) collective-permute-start(bf16[4,2,2,128,128]{4,3,2,1,0:T(8,128)(2,1)S(1)} %join.8), channel_id=1, source_target_pairs={{0,24},{1,25},{2,26},{3,27},{4,28},{5,29},{6,30},{7,31},{8,16},{9,... | collective-permute-start | bytes 1572872 | tf_op jit(solution)/shard_map/keys_y2/ppermute | solution.py:44
  68.9 1.9 %collective-permute-start.10 = (bf16[4,2,2,128,128]{4,3,2,1,0:T(8,128)(2,1)S(1)}, bf16[4,2,2,128,128]{4,3,2,1,0:T(8,128)(2,1)S(1)}, u32[]{:S(2)}, u32[]{:S(2)}) collective-permute-start(bf16[4,2,2,128,128]{4,3,2,1,0:T(8,128)(2,1)S(1)} %collective-permute-done.8.refs_0_), channel_id=1, source_target_pairs={{0,32},{1,33},{2,34},{3,35},{4,36},{5,37},{6,38},{7,39},{8,40},{9,... | collective-permute-start | bytes 1572872 | tf_op jit(solution)/shard_map/keys_c1/ppermute | solution.py:44
  70.8 1.1 %one.1 = (f32[4,1,1024]{2,1,0:T(1,128)S(1)}, f32[4,1,1024]{2,1,0:T(1,128)S(1)}, f32[4,128,1024]{2,1,0:T(8,128)S(1)}) custom-call(s32[1]{0:T(128)} %bitcast.cd, s32[16]{0:T(128)S(1)} %copy-done.1, s32[16]{0:T(128)S(1)} %get-tuple-element.47.info, bf16[4,2,2,128,128]{4,3,2,1,0:T(8,128)(2,1)S(1)} %join.9.refs_0_, ...), custom_call_target="tpu_custom_call" | custom-call | flops 1048576 | bytes 1024 | tf_op jit(solution)/shard_map/one/pallas_call | solution.py:309
  72.0 2.6 %other.1 = (f32[4,1,1024]{2,1,0:T(1,128)S(1)}, f32[4,1,1024]{2,1,0:T(1,128)S(1)}, f32[4,128,1024]{2,1,0:T(8,128)S(1)}) custom-call(s32[1]{0:T(128)} %bitcast.cd, s32[16]{0:T(128)S(1)} %copy-done.1, s32[16]{0:T(128)S(1)} %get-tuple-element.47.info, bf16[4,2,2,128,128]{4,3,2,1,0:T(8,128)(2,1)S(1)} %collective-permute-done.11.refs_0_, ...), custom_call_target="tpu_custom_call" | custom-call | flops 1048576 | bytes 1024 | tf_op jit(solution)/shard_map/other/pallas_call | solution.py:309
  74.5 2.1 %collective-permute-done.9.refs_1_ = bf16[4,2,2,128,128]{4,3,2,1,0:T(8,128)(2,1)S(1)} collective-permute-done((bf16[4,2,2,128,128]{4,3,2,1,0:T(8,128)(2,1)S(1)}, bf16[4,2,2,128,128]{4,3,2,1,0:T(8,128)(2,1)S(1)}, u32[]{:S(2)}, u32[]{:S(2)}) %collective-permute-start.9) | collective-permute-done | bytes 524320 | tf_op jit(solution)/shard_map/keys_y2/ppermute | solution.py:44
  76.6 2.1 %collective-permute-start.13 = (bf16[4,2,2,128,128]{4,3,2,1,0:T(8,128)(2,1)S(1)}, bf16[4,2,2,128,128]{4,3,2,1,0:T(8,128)(2,1)S(1)}, u32[]{:S(2)}, u32[]{:S(2)}) collective-permute-start(bf16[4,2,2,128,128]{4,3,2,1,0:T(8,128)(2,1)S(1)} %collective-permute-done.9.refs_1_), channel_id=1, source_target_pairs={{0,32},{1,33},{2,34},{3,35},{4,36},{5,37},{6,38},{7,39},{8,40},{9,... | collective-permute-start | bytes 1572872 | tf_op jit(solution)/shard_map/keys_c2/ppermute | solution.py:44
  78.7 1.4 %far.1 = (f32[4,1,1024]{2,1,0:T(1,128)S(1)}, f32[4,1,1024]{2,1,0:T(1,128)S(1)}, f32[4,128,1024]{2,1,0:T(8,128)S(1)}) custom-call(s32[1]{0:T(128)} %bitcast.cd, s32[16]{0:T(128)S(1)} %copy-done.1, s32[16]{0:T(128)S(1)} %get-tuple-element.47.info, bf16[4,2,2,128,128]{4,3,2,1,0:T(8,128)(2,1)S(1)} %collective-permute-done.8.refs_0_, ...), custom_call_target="tpu_custom_call" | custom-call | flops 1048576 | bytes 1024 | tf_op jit(solution)/shard_map/far/pallas_call | solution.py:309
  80.4 1.5 %last.2 = bf16[144,1024]{1,0:T(8,128)(2,1)S(1)} custom-call(s32[1]{0:T(128)} %bitcast.cd, s32[16]{0:T(128)S(1)} %copy-done.1, s32[16]{0:T(128)S(1)} %get-tuple-element.47.info, bf16[4,2,2,128,128]{4,3,2,1,0:T(8,128)(2,1)S(1)} %collective-permute-done.10.refs_0_, bf16[4,2,2,128,128]{4,3,2,1,0:T(8,128)(2,1)S(1)} %collective-permute-done.13.refs_1_, ...), custom_call_target="tpu_custom_call" | custom-call | flops 1048576 | bytes 1024 | tf_op jit(solution)/shard_map/last/pallas_call | solution.py:309
  81.9 6.3 %collective-permute-start.16 = (bf16[144,1024]{1,0:T(8,128)(2,1)S(1)}, bf16[144,1024]{1,0:T(8,128)(2,1)S(1)}, u32[]{:S(2)}, u32[]{:S(2)}) collective-permute-start(bf16[144,1024]{1,0:T(8,128)(2,1)S(1)} %last.2), channel_id=1, source_target_pairs={{0,65},{1,64},{2,67},{3,66},{4,69},{5,68},{6,71},{7,70},{8,73},{9,... | collective-permute-start | bytes 884744 | tf_op jit(solution)/shard_map/sums/ppermute | solution.py:44
  88.2 2.3 %last.3 = (bf16[144,1024]{1,0:T(8,128)(2,1)S(1)}, bf16[144,1024]{1,0:T(8,128)(2,1)S(1)}) custom-call(s32[1]{0:T(128)} %bitcast.cd, s32[16]{0:T(128)S(1)} %copy-done.1, s32[16]{0:T(128)S(1)} %get-tuple-element.47.info, bf16[4,2,2,128,128]{4,3,2,1,0:T(8,128)(2,1)S(1)} %collective-permute-done.10.refs_0_, ...), custom_call_target="tpu_custom_call" | custom-call | flops 1048576 | bytes 1024 | tf_op jit(solution)/shard_map/last/pallas_call | solution.py:309
  90.6 2.4 %collective-permute-start.14 = (bf16[144,1024]{1,0:T(8,128)(2,1)S(1)}, bf16[144,1024]{1,0:T(8,128)(2,1)S(1)}, u32[]{:S(2)}, u32[]{:S(2)}) collective-permute-start(bf16[144,1024]{1,0:T(8,128)(2,1)S(1)} %get-tuple-element.78), channel_id=1, source_target_pairs={{0,64},{1,65},{2,66},{3,67},{4,68},{5,69},{6,70},{7,71},{8,72},{9,... | collective-permute-start | bytes 884744 | tf_op jit(solution)/shard_map/sums/ppermute | solution.py:44
  93.0 2.2 %collective-permute-start.15 = (bf16[144,1024]{1,0:T(8,128)(2,1)S(1)}, bf16[144,1024]{1,0:T(8,128)(2,1)S(1)}, u32[]{:S(2)}, u32[]{:S(2)}) collective-permute-start(bf16[144,1024]{1,0:T(8,128)(2,1)S(1)} %get-tuple-element.79), channel_id=1, source_target_pairs={{0,1},{1,0},{2,3},{3,2},{4,5},{5,4},{6,7},{7,6},{8,9},{9,8},{10,11... | collective-permute-start | bytes 884744 | tf_op jit(solution)/shard_map/sums/ppermute | solution.py:44
  95.4 1.5 %final.1 = (f32[1,1,1024]{2,1,0:T(1,128)S(1)}, f32[1,1,1024]{2,1,0:T(1,128)S(1)}, f32[1,128,1024]{2,1,0:T(8,128)S(1)}) custom-call(s32[1]{0:T(128)} %bitcast.cd, s32[16]{0:T(128)S(1)} %copy-done.1, s32[16]{0:T(128)S(1)} %get-tuple-element.47.info, bf16[4,2,2,128,128]{4,3,2,1,0:T(8,128)(2,1)S(1)} %collective-permute-done.10.refs_0_, ...), custom_call_target="tpu_custom_call" | custom-call | flops 8589934592 | bytes 8388608 | tf_op jit(solution)/shard_map/final/pallas_call | solution.py:309
  96.9 4.8 %collective-permute-done.14.a_ref = bf16[144,1024]{1,0:T(8,128)(2,1)S(1)} collective-permute-done((bf16[144,1024]{1,0:T(8,128)(2,1)S(1)}, bf16[144,1024]{1,0:T(8,128)(2,1)S(1)}, u32[]{:S(2)}, u32[]{:S(2)}) %collective-permute-start.14) | collective-permute-done | bytes 294944 | tf_op jit(solution)/shard_map/sums/ppermute | solution.py:44
  101.7 2.4 %collective-permute-done.15.b_ref = bf16[144,1024]{1,0:T(8,128)(2,1)S(1)} collective-permute-done((bf16[144,1024]{1,0:T(8,128)(2,1)S(1)}, bf16[144,1024]{1,0:T(8,128)(2,1)S(1)}, u32[]{:S(2)}, u32[]{:S(2)}) %collective-permute-start.15) | collective-permute-done | bytes 294944 | tf_op jit(solution)/shard_map/sums/ppermute | solution.py:44
  104.1 0.9 combine.1
  (23 shorter events, 1.9 us)
Async XLA Ops:
  0.8 17.4 %collective-permute-start.1 = (bf16[2,128,128]{2,1,0:T(8,128)(2,1)S(1)}, bf16[2,128,128]{2,1,0:T(8,128)(2,1)S(1)}, u32[]{:S(2)}, u32[]{:S(2)}) collective-permute-start(bf16[2,128,128]{2,1,0:T(8,128)(2,1)S(1)} %pad_maximum_fusion.1), channel_id=1, source_target_pairs={{0,128},{1,129},{2,130},{3,131},{4,132},{5,133},{6,134},{7,135},{8... | collective-permute-start | bytes 196616 | tf_op jit(solution)/shard_map/keys_x/ppermute | solution.py:44
  12.6 5.6 %collective-permute-start = (bf16[2,128,128]{2,1,0:T(8,128)(2,1)S(1)}, bf16[2,128,128]{2,1,0:T(8,128)(2,1)S(1)}, u32[]{:S(2)}, u32[]{:S(2)}) collective-permute-start(bf16[2,128,128]{2,1,0:T(8,128)(2,1)S(1)} %pad_maximum_fusion.1), channel_id=1, source_target_pairs={{0,0},{1,1},{2,2},{3,3},{4,4},{5,5},{6,6},{7,7},{8,72},{9,73},{10,... | collective-permute-start | bytes 196616 | tf_op jit(solution)/shard_map/keys_x/ppermute | solution.py:44
  15.1 26.8 %copy-start = (bf16[144,1024]{1,0:T(8,128)(2,1)S(1)}, bf16[144,1024]{1,0:T(8,128)(2,1)}, u32[]{:S(2)}) copy-start(bf16[144,1024]{1,0:T(8,128)(2,1)} %prep.1.refs_1_) | copy-start | bytes 884740
  15.1 26.8 %collective-permute-start.5 = (bf16[144,1024]{1,0:T(8,128)(2,1)}, bf16[144,1024]{1,0:T(8,128)(2,1)S(1)}, u32[]{:S(2)}, u32[]{:S(2)}) collective-permute-start(bf16[144,1024]{1,0:T(8,128)(2,1)} %prep.1.refs_1_), channel_id=1, source_target_pairs={{0,1},{1,0},{2,3},{3,2},{4,5},{5,4},{6,7},{7,6},{8,9},{9,8},{10,11... | collective-permute-start | bytes 884744 | tf_op jit(solution)/shard_map/queries_z/ppermute | solution.py:44
  18.3 10.9 %collective-permute-start.2 = (bf16[1,2,2,128,128]{4,3,2,1,0:T(8,128)(2,1)S(1)}, bf16[1,2,2,128,128]{4,3,2,1,0:T(8,128)(2,1)S(1)}, u32[]{:S(2)}, u32[]{:S(2)}) collective-permute-start(bf16[1,2,2,128,128]{4,3,2,1,0:T(8,128)(2,1)S(1)} %pair.1.refs_0_), channel_id=1, source_target_pairs={{0,4},{1,5},{2,6},{3,7},{4,0},{5,1},{6,2},{7,3},{8,12},{9,13},{10,... | collective-permute-start | bytes 393224 | tf_op jit(solution)/shard_map/keys_z1/ppermute | solution.py:44
  29.2 16.5 %collective-permute-start.3 = (bf16[2,2,2,128,128]{4,3,2,1,0:T(8,128)(2,1)S(1)}, bf16[2,2,2,128,128]{4,3,2,1,0:T(8,128)(2,1)S(1)}, u32[]{:S(2)}, u32[]{:S(2)}) collective-permute-start(bf16[2,2,2,128,128]{4,3,2,1,0:T(8,128)(2,1)S(1)} %join.5.refs_0_), channel_id=1, source_target_pairs={{0,2},{1,3},{2,0},{3,1},{4,6},{5,7},{6,4},{7,5},{8,10},{9,11},{10,... | collective-permute-start | bytes 786440 | tf_op jit(solution)/shard_map/keys_z2/ppermute | solution.py:44
  36.0 10.2 %collective-permute-start.4 = (bf16[2,2,2,128,128]{4,3,2,1,0:T(8,128)(2,1)S(1)}, bf16[2,2,2,128,128]{4,3,2,1,0:T(8,128)(2,1)S(1)}, u32[]{:S(2)}, u32[]{:S(2)}) collective-permute-start(bf16[2,2,2,128,128]{4,3,2,1,0:T(8,128)(2,1)S(1)} %join.5.refs_0_), channel_id=1, source_target_pairs={{0,8},{1,9},{2,10},{3,11},{4,12},{5,13},{6,14},{7,15},{8,0},{9,1},... | collective-permute-start | bytes 786440 | tf_op jit(solution)/shard_map/keys_y1/ppermute | solution.py:44
  42.8 16.2 %copy-start.1 = (s32[16]{0:T(128)S(1)}, s32[16]{0:T(128)}, u32[]{:S(2)}) copy-start(s32[16]{0:T(128)} %lengths.13) | copy-start | bytes 196
  42.8 16.2 %collective-permute-start.6 = (bf16[2,144,1024]{2,1,0:T(8,128)(2,1)}, bf16[2,144,1024]{2,1,0:T(8,128)(2,1)S(1)}, u32[]{:S(2)}, u32[]{:S(2)}) collective-permute-start(bf16[2,144,1024]{2,1,0:T(8,128)(2,1)} %pad_maximum_fusion), channel_id=1, source_target_pairs={{0,64},{1,65},{2,66},{3,67},{4,68},{5,69},{6,70},{7,71},{8,72},{9,... | collective-permute-start | bytes 1769480 | tf_op jit(solution)/shard_map/queries_x/ppermute | solution.py:44
  46.2 16.1 %collective-permute-start.8 = (bf16[4,2,2,128,128]{4,3,2,1,0:T(8,128)(2,1)S(1)}, bf16[4,2,2,128,128]{4,3,2,1,0:T(8,128)(2,1)S(1)}, u32[]{:S(2)}, u32[]{:S(2)}) collective-permute-start(bf16[4,2,2,128,128]{4,3,2,1,0:T(8,128)(2,1)S(1)} %join.7), channel_id=1, source_target_pairs={{0,24},{1,25},{2,26},{3,27},{4,28},{5,29},{6,30},{7,31},{8,16},{9,... | collective-permute-start | bytes 1572872 | tf_op jit(solution)/shard_map/keys_y2/ppermute | solution.py:44
  51.6 10.7 %collective-permute-start.7 = (bf16[2,2,2,128,128]{4,3,2,1,0:T(8,128)(2,1)S(1)}, bf16[2,2,2,128,128]{4,3,2,1,0:T(8,128)(2,1)S(1)}, u32[]{:S(2)}, u32[]{:S(2)}) collective-permute-start(bf16[2,2,2,128,128]{4,3,2,1,0:T(8,128)(2,1)S(1)} %collective-permute-done.3.refs_1_.refs_0_), channel_id=1, source_target_pairs={{0,8},{1,9},{2,10},{3,11},{4,12},{5,13},{6,14},{7,15},{8,0},{9,1},... | collective-permute-start | bytes 786440 | tf_op jit(solution)/shard_map/keys_y1/ppermute | solution.py:44
  53.5 18.4 %collective-permute-start.11 = (bf16[4,2,2,128,128]{4,3,2,1,0:T(8,128)(2,1)S(1)}, bf16[4,2,2,128,128]{4,3,2,1,0:T(8,128)(2,1)S(1)}, u32[]{:S(2)}, u32[]{:S(2)}) collective-permute-start(bf16[4,2,2,128,128]{4,3,2,1,0:T(8,128)(2,1)S(1)} %join.6.refs_0_), channel_id=1, source_target_pairs={{0,32},{1,33},{2,34},{3,35},{4,36},{5,37},{6,38},{7,39},{8,40},{9,... | collective-permute-start | bytes 1572872 | tf_op jit(solution)/shard_map/keys_c1/ppermute | solution.py:44
  62.4 9.6 %collective-permute-start.12 = (bf16[4,2,2,128,128]{4,3,2,1,0:T(8,128)(2,1)S(1)}, bf16[4,2,2,128,128]{4,3,2,1,0:T(8,128)(2,1)S(1)}, u32[]{:S(2)}, u32[]{:S(2)}) collective-permute-start(bf16[4,2,2,128,128]{4,3,2,1,0:T(8,128)(2,1)S(1)} %join.9.refs_0_), channel_id=1, source_target_pairs={{0,32},{1,33},{2,34},{3,35},{4,36},{5,37},{6,38},{7,39},{8,40},{9,... | collective-permute-start | bytes 1572872 | tf_op jit(solution)/shard_map/keys_c1/ppermute | solution.py:44
  64.3 12.3 %collective-permute-start.9 = (bf16[4,2,2,128,128]{4,3,2,1,0:T(8,128)(2,1)S(1)}, bf16[4,2,2,128,128]{4,3,2,1,0:T(8,128)(2,1)S(1)}, u32[]{:S(2)}, u32[]{:S(2)}) collective-permute-start(bf16[4,2,2,128,128]{4,3,2,1,0:T(8,128)(2,1)S(1)} %join.8), channel_id=1, source_target_pairs={{0,24},{1,25},{2,26},{3,27},{4,28},{5,29},{6,30},{7,31},{8,16},{9,... | collective-permute-start | bytes 1572872 | tf_op jit(solution)/shard_map/keys_y2/ppermute | solution.py:44
  68.9 7.7 %collective-permute-start.10 = (bf16[4,2,2,128,128]{4,3,2,1,0:T(8,128)(2,1)S(1)}, bf16[4,2,2,128,128]{4,3,2,1,0:T(8,128)(2,1)S(1)}, u32[]{:S(2)}, u32[]{:S(2)}) collective-permute-start(bf16[4,2,2,128,128]{4,3,2,1,0:T(8,128)(2,1)S(1)} %collective-permute-done.8.refs_0_), channel_id=1, source_target_pairs={{0,32},{1,33},{2,34},{3,35},{4,36},{5,37},{6,38},{7,39},{8,40},{9,... | collective-permute-start | bytes 1572872 | tf_op jit(solution)/shard_map/keys_c1/ppermute | solution.py:44
  76.6 3.8 %collective-permute-start.13 = (bf16[4,2,2,128,128]{4,3,2,1,0:T(8,128)(2,1)S(1)}, bf16[4,2,2,128,128]{4,3,2,1,0:T(8,128)(2,1)S(1)}, u32[]{:S(2)}, u32[]{:S(2)}) collective-permute-start(bf16[4,2,2,128,128]{4,3,2,1,0:T(8,128)(2,1)S(1)} %collective-permute-done.9.refs_1_), channel_id=1, source_target_pairs={{0,32},{1,33},{2,34},{3,35},{4,36},{5,37},{6,38},{7,39},{8,40},{9,... | collective-permute-start | bytes 1572872 | tf_op jit(solution)/shard_map/keys_c2/ppermute | solution.py:44
  81.9 13.5 %collective-permute-start.16 = (bf16[144,1024]{1,0:T(8,128)(2,1)S(1)}, bf16[144,1024]{1,0:T(8,128)(2,1)S(1)}, u32[]{:S(2)}, u32[]{:S(2)}) collective-permute-start(bf16[144,1024]{1,0:T(8,128)(2,1)S(1)} %last.2), channel_id=1, source_target_pairs={{0,65},{1,64},{2,67},{3,66},{4,69},{5,68},{6,71},{7,70},{8,73},{9,... | collective-permute-start | bytes 884744 | tf_op jit(solution)/shard_map/sums/ppermute | solution.py:44
  90.6 11.1 %collective-permute-start.14 = (bf16[144,1024]{1,0:T(8,128)(2,1)S(1)}, bf16[144,1024]{1,0:T(8,128)(2,1)S(1)}, u32[]{:S(2)}, u32[]{:S(2)}) collective-permute-start(bf16[144,1024]{1,0:T(8,128)(2,1)S(1)} %get-tuple-element.78), channel_id=1, source_target_pairs={{0,64},{1,65},{2,66},{3,67},{4,68},{5,69},{6,70},{7,71},{8,72},{9,... | collective-permute-start | bytes 884744 | tf_op jit(solution)/shard_map/sums/ppermute | solution.py:44
  93.0 11.1 %collective-permute-start.15 = (bf16[144,1024]{1,0:T(8,128)(2,1)S(1)}, bf16[144,1024]{1,0:T(8,128)(2,1)S(1)}, u32[]{:S(2)}, u32[]{:S(2)}) collective-permute-start(bf16[144,1024]{1,0:T(8,128)(2,1)S(1)} %get-tuple-element.79), channel_id=1, source_target_pairs={{0,1},{1,0},{2,3},{3,2},{4,5},{5,4},{6,7},{7,6},{8,9},{9,8},{10,11... | collective-permute-start | bytes 884744 | tf_op jit(solution)/shard_map/sums/ppermute | solution.py:44
where the time goes:
time: 106 us; the launch traced here: 105 us
  starting transfers between devices  71.2 us (67%)
  Pallas kernels  16.7 us (16%)
  waiting for transfers between devices  15.1 us (14%)
  other arithmetic  1.66 us (2%)
    ppermute x17, starting transfers between devices, move(): return lax.ppermute(x, AXES, pairs)  71.2 us
    ppermute x17, waiting for transfers between devices, move(): return lax.ppermute(x, AXES, pairs)  15.1 us
    pallas_call x14, Pallas kernels, call(): pl.pallas_call(kernel, out_shape=out_shape, in_specs=[SMEM] * len(scalars...  14.9 us
  transfers between devices with their start and end apart: 17, of which 8 were waited for; matrix products, arithmetic and copies ran while one was open for 1% of the time, Pallas kernels for 14%

commit v1 on v0

--- a/solution.py
+++ b/solution.py
@@ -339,12 +339,13 @@
     qt = pl.pallas_call(prep_kernel, out_shape=PACKED, in_specs=[VMEM] * 2, out_specs=VMEM, name="prep")(
         queries, keys
     )
-    with jax.named_scope("queries_z"):
-        qz = move(qt, to_slot(1))
 
     with jax.named_scope("keys_x"):
         before = move(raw, to_next_span)
         mine = move(raw, lambda xp, y, **_: dict(xp=xp ^ (y & 1)))
+        mine, before, qt = lax.optimization_barrier((mine, before, qt))
+    with jax.named_scope("queries_z"):
+        qz = move(qt, to_slot(1))
     with jax.named_scope("keys_z1"):
         shape = jax.ShapeDtypeStruct((1, 2, 2, TOKENS, HEAD), jnp.bfloat16)
         held = call(pair_kernel, "pair", shape, (), [mine, before], VMEM, LONG)
@@ -358,7 +359,7 @@
         return move(x, lambda y, c, **_: dict(y=y ^ 1 if c else 3 - y))
 
     with jax.named_scope("keys_z2"):
-        half = join(held, got)
+        half = join(held, got, cost=LONG)
         rest = move(half, lambda w, c, **_: dict(w=w ^ (2 if c else 1)))
     with jax.named_scope("keys_y1"):
         one_half = along_y1(half)

time: 106 us -> 108 us (1.019)
  the two profiles are of different devices: /device:TPU:4 before, /device:TPU:320 now
where the time goes in v1:
time: 108 us
  starting transfers between devices  51.6 us (48%)
  Pallas kernels  27.5 us (25%)
  waiting for transfers between devices  27.1 us (25%)
  other arithmetic  1.66 us (2%)
    ppermute x17, starting transfers between devices, move(): return lax.ppermute(x, AXES, pairs)  51.6 us
    ppermute x17, waiting for transfers between devices, move(): return lax.ppermute(x, AXES, pairs)  27.1 us
    pallas_call x14, Pallas kernels, call(): pl.pallas_call(kernel, out_shape=out_shape, in_specs=[SMEM] * len(scalars...  25.6 us
  transfers between devices with their start and end apart: 17, of which 8 were waited for; matrix products, arithmetic and copies ran while one was open for 1% of the time, Pallas kernels for 23%

profile of v1, /device:TPU:320, one launch (start us, length us, event | category | flops | bytes accessed | tf_op | source)
XLA Modules:
  0.0 108.1 jit_solution(8631306249549231683)
XLA Ops:
  0.8 4.9 %collective-permute-start.1 = (bf16[2,128,128]{2,1,0:T(8,128)(2,1)S(1)}, bf16[2,128,128]{2,1,0:T(8,128)(2,1)S(1)}, u32[]{:S(2)}, u32[]{:S(2)}) collective-permute-start(bf16[2,128,128]{2,1,0:T(8,128)(2,1)S(1)} %pad_maximum_fusion.1), channel_id=1, source_target_pairs={{0,128},{1,129},{2,130},{3,131},{4,132},{5,133},{6,134},{7,135},{8... | collective-permute-start | bytes 196616 | tf_op jit(solution)/shard_map/keys_x/ppermute | solution.py:44
  6.4 1.9 %prep.1.refs_1_ = bf16[144,1024]{1,0:T(8,128)(2,1)} custom-call(bf16[128,1024]{1,0:T(8,128)(2,1)} %q_ref.1, bf16[128,128]{1,0:T(8,128)(2,1)} %k_ref.1), custom_call_target="tpu_custom_call" | custom-call | tf_op jit(solution)/shard_map/prep/pallas_call | solution.py:339
  8.3 6.8 %collective-permute-done.1.b_ref = bf16[2,128,128]{2,1,0:T(8,128)(2,1)S(1)} collective-permute-done((bf16[2,128,128]{2,1,0:T(8,128)(2,1)S(1)}, bf16[2,128,128]{2,1,0:T(8,128)(2,1)S(1)}, u32[]{:S(2)}, u32[]{:S(2)}) %collective-permute-start.1) | collective-permute-done | bytes 65568 | tf_op jit(solution)/shard_map/keys_x/ppermute | solution.py:44
  15.2 4.5 %collective-permute-start.2 = (bf16[1,2,2,128,128]{4,3,2,1,0:T(8,128)(2,1)S(1)}, bf16[1,2,2,128,128]{4,3,2,1,0:T(8,128)(2,1)S(1)}, u32[]{:S(2)}, u32[]{:S(2)}) collective-permute-start(bf16[1,2,2,128,128]{4,3,2,1,0:T(8,128)(2,1)S(1)} %pair.1.refs_0_), channel_id=1, source_target_pairs={{0,4},{1,5},{2,6},{3,7},{4,0},{5,1},{6,2},{7,3},{8,12},{9,13},{10,... | collective-permute-start | bytes 393224 | tf_op jit(solution)/shard_map/keys_z1/ppermute | solution.py:44
  19.7 1.9 %collective-permute-start.5 = (bf16[144,1024]{1,0:T(8,128)(2,1)S(1)}, bf16[144,1024]{1,0:T(8,128)(2,1)S(1)}, u32[]{:S(2)}, u32[]{:S(2)}) collective-permute-start(bf16[144,1024]{1,0:T(8,128)(2,1)S(1)} %copy-done), channel_id=1, source_target_pairs={{0,1},{1,0},{2,3},{3,2},{4,5},{5,4},{6,7},{7,6},{8,9},{9,8},{10,11... | collective-permute-start | bytes 884744 | tf_op jit(solution)/shard_map/queries_z/ppermute | solution.py:44
  21.6 9.2 %collective-permute-done.2.refs_1_ = bf16[1,2,2,128,128]{4,3,2,1,0:T(8,128)(2,1)S(1)} collective-permute-done((bf16[1,2,2,128,128]{4,3,2,1,0:T(8,128)(2,1)S(1)}, bf16[1,2,2,128,128]{4,3,2,1,0:T(8,128)(2,1)S(1)}, u32[]{:S(2)}, u32[]{:S(2)}) %collective-permute-start.2) | collective-permute-done | bytes 131104 | tf_op jit(solution)/shard_map/keys_z1/ppermute | solution.py:44
  30.8 1.9 %collective-permute-start.3 = (bf16[2,2,2,128,128]{4,3,2,1,0:T(8,128)(2,1)S(1)}, bf16[2,2,2,128,128]{4,3,2,1,0:T(8,128)(2,1)S(1)}, u32[]{:S(2)}, u32[]{:S(2)}) collective-permute-start(bf16[2,2,2,128,128]{4,3,2,1,0:T(8,128)(2,1)S(1)} %join.5.refs_0_), channel_id=1, source_target_pairs={{0,2},{1,3},{2,0},{3,1},{4,6},{5,7},{6,4},{7,5},{8,10},{9,11},{10,... | collective-permute-start | bytes 786440 | tf_op jit(solution)/shard_map/keys_z2/ppermute | solution.py:44
  32.8 3.2 %collective-permute-start.4 = (bf16[2,2,2,128,128]{4,3,2,1,0:T(8,128)(2,1)S(1)}, bf16[2,2,2,128,128]{4,3,2,1,0:T(8,128)(2,1)S(1)}, u32[]{:S(2)}, u32[]{:S(2)}) collective-permute-start(bf16[2,2,2,128,128]{4,3,2,1,0:T(8,128)(2,1)S(1)} %join.5.refs_0_), channel_id=1, source_target_pairs={{0,8},{1,9},{2,10},{3,11},{4,12},{5,13},{6,14},{7,15},{8,0},{9,1},... | collective-permute-start | bytes 786440 | tf_op jit(solution)/shard_map/keys_y1/ppermute | solution.py:44
  36.0 2.7 %collective-permute-done.5.refs_2_ = bf16[144,1024]{1,0:T(8,128)(2,1)S(1)} collective-permute-done((bf16[144,1024]{1,0:T(8,128)(2,1)S(1)}, bf16[144,1024]{1,0:T(8,128)(2,1)S(1)}, u32[]{:S(2)}, u32[]{:S(2)}) %collective-permute-start.5) | collective-permute-done | bytes 294944 | tf_op jit(solution)/shard_map/queries_z/ppermute | solution.py:44
  39.6 3.6 %collective-permute-start.6 = (bf16[2,144,1024]{2,1,0:T(8,128)(2,1)}, bf16[2,144,1024]{2,1,0:T(8,128)(2,1)S(1)}, u32[]{:S(2)}, u32[]{:S(2)}) collective-permute-start(bf16[2,144,1024]{2,1,0:T(8,128)(2,1)} %pad_maximum_fusion), channel_id=1, source_target_pairs={{0,64},{1,65},{2,66},{3,67},{4,68},{5,69},{6,70},{7,71},{8,72},{9,... | collective-permute-start | bytes 1769480 | tf_op jit(solution)/shard_map/queries_x/ppermute | solution.py:44
  43.2 1.9 %collective-permute-done.3.refs_1_.refs_0_ = bf16[2,2,2,128,128]{4,3,2,1,0:T(8,128)(2,1)S(1)} collective-permute-done((bf16[2,2,2,128,128]{4,3,2,1,0:T(8,128)(2,1)S(1)}, bf16[2,2,2,128,128]{4,3,2,1,0:T(8,128)(2,1)S(1)}, u32[]{:S(2)}, u32[]{:S(2)}) %collective-permute-start.3) | collective-permute-done | bytes 262176 | tf_op jit(solution)/shard_map/keys_z2/ppermute | solution.py:44
  45.2 4.7 %collective-permute-start.8 = (bf16[4,2,2,128,128]{4,3,2,1,0:T(8,128)(2,1)S(1)}, bf16[4,2,2,128,128]{4,3,2,1,0:T(8,128)(2,1)S(1)}, u32[]{:S(2)}, u32[]{:S(2)}) collective-permute-start(bf16[4,2,2,128,128]{4,3,2,1,0:T(8,128)(2,1)S(1)} %join.7), channel_id=1, source_target_pairs={{0,24},{1,25},{2,26},{3,27},{4,28},{5,29},{6,30},{7,31},{8,16},{9,... | collective-permute-start | bytes 1572872 | tf_op jit(solution)/shard_map/keys_y2/ppermute | solution.py:44
  49.9 2.3 %collective-permute-start.7 = (bf16[2,2,2,128,128]{4,3,2,1,0:T(8,128)(2,1)S(1)}, bf16[2,2,2,128,128]{4,3,2,1,0:T(8,128)(2,1)S(1)}, u32[]{:S(2)}, u32[]{:S(2)}) collective-permute-start(bf16[2,2,2,128,128]{4,3,2,1,0:T(8,128)(2,1)S(1)} %collective-permute-done.3.refs_1_.refs_0_), channel_id=1, source_target_pairs={{0,8},{1,9},{2,10},{3,11},{4,12},{5,13},{6,14},{7,15},{8,0},{9,1},... | collective-permute-start | bytes 786440 | tf_op jit(solution)/shard_map/keys_y1/ppermute | solution.py:44
  52.2 1.9 %collective-permute-start.11 = (bf16[4,2,2,128,128]{4,3,2,1,0:T(8,128)(2,1)S(1)}, bf16[4,2,2,128,128]{4,3,2,1,0:T(8,128)(2,1)S(1)}, u32[]{:S(2)}, u32[]{:S(2)}) collective-permute-start(bf16[4,2,2,128,128]{4,3,2,1,0:T(8,128)(2,1)S(1)} %join.6.refs_0_), channel_id=1, source_target_pairs={{0,32},{1,33},{2,34},{3,35},{4,36},{5,37},{6,38},{7,39},{8,40},{9,... | collective-permute-start | bytes 1572872 | tf_op jit(solution)/shard_map/keys_c1/ppermute | solution.py:44
  54.2 4.6 %own.1 = (s32[16]{0:T(128)S(1)}, bf16[4,144,1024]{2,1,0:T(8,128)(2,1)S(1)}, f32[4,1,1024]{2,1,0:T(1,128)S(1)}, f32[4,1,1024]{2,1,0:T(1,128)S(1)}, f32[4,128,1024]{2,1,0:T(8,128)S(1)}) custom-call(s32[1]{0:T(128)} %bitcast.cd, s32[16]{0:T(128)S(1)} %copy-done.1, bf16[4,2,2,128,128]{4,3,2,1,0:T(8,128)(2,1)S(1)} %join.6.refs_0_, bf16[144,1024]{1,0:T(8,128)(2,1)S(1)} %copy-done, ...), custom_call_target="tpu_custom_call" | custom-call | flops 1048576 | bytes 1024 | tf_op jit(solution)/shard_map/own/pallas_call | solution.py:309
  58.8 1.3 %collective-permute-done.8.refs_0_ = bf16[4,2,2,128,128]{4,3,2,1,0:T(8,128)(2,1)S(1)} collective-permute-done((bf16[4,2,2,128,128]{4,3,2,1,0:T(8,128)(2,1)S(1)}, bf16[4,2,2,128,128]{4,3,2,1,0:T(8,128)(2,1)S(1)}, u32[]{:S(2)}, u32[]{:S(2)}) %collective-permute-start.8) | collective-permute-done | bytes 524320 | tf_op jit(solution)/shard_map/keys_y2/ppermute | solution.py:44
  60.1 1.9 %collective-permute-start.12 = (bf16[4,2,2,128,128]{4,3,2,1,0:T(8,128)(2,1)S(1)}, bf16[4,2,2,128,128]{4,3,2,1,0:T(8,128)(2,1)S(1)}, u32[]{:S(2)}, u32[]{:S(2)}) collective-permute-start(bf16[4,2,2,128,128]{4,3,2,1,0:T(8,128)(2,1)S(1)} %join.9.refs_0_), channel_id=1, source_target_pairs={{0,32},{1,33},{2,34},{3,35},{4,36},{5,37},{6,38},{7,39},{8,40},{9,... | collective-permute-start | bytes 1572872 | tf_op jit(solution)/shard_map/keys_c1/ppermute | solution.py:44
  62.1 4.4 %collective-permute-start.9 = (bf16[4,2,2,128,128]{4,3,2,1,0:T(8,128)(2,1)S(1)}, bf16[4,2,2,128,128]{4,3,2,1,0:T(8,128)(2,1)S(1)}, u32[]{:S(2)}, u32[]{:S(2)}) collective-permute-start(bf16[4,2,2,128,128]{4,3,2,1,0:T(8,128)(2,1)S(1)} %join.8), channel_id=1, source_target_pairs={{0,24},{1,25},{2,26},{3,27},{4,28},{5,29},{6,30},{7,31},{8,16},{9,... | collective-permute-start | bytes 1572872 | tf_op jit(solution)/shard_map/keys_y2/ppermute | solution.py:44
  66.5 1.9 %collective-permute-start.10 = (bf16[4,2,2,128,128]{4,3,2,1,0:T(8,128)(2,1)S(1)}, bf16[4,2,2,128,128]{4,3,2,1,0:T(8,128)(2,1)S(1)}, u32[]{:S(2)}, u32[]{:S(2)}) collective-permute-start(bf16[4,2,2,128,128]{4,3,2,1,0:T(8,128)(2,1)S(1)} %collective-permute-done.8.refs_0_), channel_id=1, source_target_pairs={{0,32},{1,33},{2,34},{3,35},{4,36},{5,37},{6,38},{7,39},{8,40},{9,... | collective-permute-start | bytes 1572872 | tf_op jit(solution)/shard_map/keys_c1/ppermute | solution.py:44
  68.4 3.6 %one.1 = (f32[4,1,1024]{2,1,0:T(1,128)S(1)}, f32[4,1,1024]{2,1,0:T(1,128)S(1)}, f32[4,128,1024]{2,1,0:T(8,128)S(1)}) custom-call(s32[1]{0:T(128)} %bitcast.cd, s32[16]{0:T(128)S(1)} %copy-done.1, s32[16]{0:T(128)S(1)} %get-tuple-element.53.info, bf16[4,2,2,128,128]{4,3,2,1,0:T(8,128)(2,1)S(1)} %join.9.refs_0_, ...), custom_call_target="tpu_custom_call" | custom-call | flops 1048576 | bytes 1024 | tf_op jit(solution)/shard_map/one/pallas_call | solution.py:309
  72.0 4.9 %other.1 = (f32[4,1,1024]{2,1,0:T(1,128)S(1)}, f32[4,1,1024]{2,1,0:T(1,128)S(1)}, f32[4,128,1024]{2,1,0:T(8,128)S(1)}) custom-call(s32[1]{0:T(128)} %bitcast.cd, s32[16]{0:T(128)S(1)} %copy-done.1, s32[16]{0:T(128)S(1)} %get-tuple-element.53.info, bf16[4,2,2,128,128]{4,3,2,1,0:T(8,128)(2,1)S(1)} %collective-permute-done.11.refs_0_, ...), custom_call_target="tpu_custom_call" | custom-call | flops 1048576 | bytes 1024 | tf_op jit(solution)/shard_map/other/pallas_call | solution.py:309
  77.0 2.1 %collective-permute-start.13 = (bf16[4,2,2,128,128]{4,3,2,1,0:T(8,128)(2,1)S(1)}, bf16[4,2,2,128,128]{4,3,2,1,0:T(8,128)(2,1)S(1)}, u32[]{:S(2)}, u32[]{:S(2)}) collective-permute-start(bf16[4,2,2,128,128]{4,3,2,1,0:T(8,128)(2,1)S(1)} %collective-permute-done.9.refs_1_), channel_id=1, source_target_pairs={{0,32},{1,33},{2,34},{3,35},{4,36},{5,37},{6,38},{7,39},{8,40},{9,... | collective-permute-start | bytes 1572872 | tf_op jit(solution)/shard_map/keys_c2/ppermute | solution.py:44
  79.1 5.0 %far.1 = (f32[4,1,1024]{2,1,0:T(1,128)S(1)}, f32[4,1,1024]{2,1,0:T(1,128)S(1)}, f32[4,128,1024]{2,1,0:T(8,128)S(1)}) custom-call(s32[1]{0:T(128)} %bitcast.cd, s32[16]{0:T(128)S(1)} %copy-done.1, s32[16]{0:T(128)S(1)} %get-tuple-element.53.info, bf16[4,2,2,128,128]{4,3,2,1,0:T(8,128)(2,1)S(1)} %collective-permute-done.8.refs_0_, ...), custom_call_target="tpu_custom_call" | custom-call | flops 1048576 | bytes 1024 | tf_op jit(solution)/shard_map/far/pallas_call | solution.py:309
  84.1 2.0 %last.2 = bf16[144,1024]{1,0:T(8,128)(2,1)S(1)} custom-call(s32[1]{0:T(128)} %bitcast.cd, s32[16]{0:T(128)S(1)} %copy-done.1, s32[16]{0:T(128)S(1)} %get-tuple-element.53.info, bf16[4,2,2,128,128]{4,3,2,1,0:T(8,128)(2,1)S(1)} %collective-permute-done.10.refs_0_, bf16[4,2,2,128,128]{4,3,2,1,0:T(8,128)(2,1)S(1)} %collective-permute-done.13.refs_1_, ...), custom_call_target="tpu_custom_call" | custom-call | flops 1048576 | bytes 1024 | tf_op jit(solution)/shard_map/last/pallas_call | solution.py:309
  86.1 5.3 %collective-permute-start.16 = (bf16[144,1024]{1,0:T(8,128)(2,1)S(1)}, bf16[144,1024]{1,0:T(8,128)(2,1)S(1)}, u32[]{:S(2)}, u32[]{:S(2)}) collective-permute-start(bf16[144,1024]{1,0:T(8,128)(2,1)S(1)} %last.2), channel_id=1, source_target_pairs={{0,65},{1,64},{2,67},{3,66},{4,69},{5,68},{6,71},{7,70},{8,73},{9,... | collective-permute-start | bytes 884744 | tf_op jit(solution)/shard_map/sums/ppermute | solution.py:44
  91.5 2.9 %last.3 = (bf16[144,1024]{1,0:T(8,128)(2,1)S(1)}, bf16[144,1024]{1,0:T(8,128)(2,1)S(1)}) custom-call(s32[1]{0:T(128)} %bitcast.cd, s32[16]{0:T(128)S(1)} %copy-done.1, s32[16]{0:T(128)S(1)} %get-tuple-element.53.info, bf16[4,2,2,128,128]{4,3,2,1,0:T(8,128)(2,1)S(1)} %collective-permute-done.10.refs_0_, ...), custom_call_target="tpu_custom_call" | custom-call | flops 1048576 | bytes 1024 | tf_op jit(solution)/shard_map/last/pallas_call | solution.py:309
  94.4 4.2 %collective-permute-start.14 = (bf16[144,1024]{1,0:T(8,128)(2,1)S(1)}, bf16[144,1024]{1,0:T(8,128)(2,1)S(1)}, u32[]{:S(2)}, u32[]{:S(2)}) collective-permute-start(bf16[144,1024]{1,0:T(8,128)(2,1)S(1)} %get-tuple-element.84), channel_id=1, source_target_pairs={{0,64},{1,65},{2,66},{3,67},{4,68},{5,69},{6,70},{7,71},{8,72},{9,... | collective-permute-start | bytes 884744 | tf_op jit(solution)/shard_map/sums/ppermute | solution.py:44
  98.6 2.2 %collective-permute-start.15 = (bf16[144,1024]{1,0:T(8,128)(2,1)S(1)}, bf16[144,1024]{1,0:T(8,128)(2,1)S(1)}, u32[]{:S(2)}, u32[]{:S(2)}) collective-permute-start(bf16[144,1024]{1,0:T(8,128)(2,1)S(1)} %get-tuple-element.85), channel_id=1, source_target_pairs={{0,1},{1,0},{2,3},{3,2},{4,5},{5,4},{6,7},{7,6},{8,9},{9,8},{10,11... | collective-permute-start | bytes 884744 | tf_op jit(solution)/shard_map/sums/ppermute | solution.py:44
  100.8 1.5 %final.1 = (f32[1,1,1024]{2,1,0:T(1,128)S(1)}, f32[1,1,1024]{2,1,0:T(1,128)S(1)}, f32[1,128,1024]{2,1,0:T(8,128)S(1)}) custom-call(s32[1]{0:T(128)} %bitcast.cd, s32[16]{0:T(128)S(1)} %copy-done.1, s32[16]{0:T(128)S(1)} %get-tuple-element.53.info, bf16[4,2,2,128,128]{4,3,2,1,0:T(8,128)(2,1)S(1)} %collective-permute-done.10.refs_0_, ...), custom_call_target="tpu_custom_call" | custom-call | flops 8589934592 | bytes 8388608 | tf_op jit(solution)/shard_map/final/pallas_call | solution.py:309
  102.2 1.4 %collective-permute-done.14.a_ref = bf16[144,1024]{1,0:T(8,128)(2,1)S(1)} collective-permute-done((bf16[144,1024]{1,0:T(8,128)(2,1)S(1)}, bf16[144,1024]{1,0:T(8,128)(2,1)S(1)}, u32[]{:S(2)}, u32[]{:S(2)}) %collective-permute-start.14) | collective-permute-done | bytes 294944 | tf_op jit(solution)/shard_map/sums/ppermute | solution.py:44
  103.6 3.6 %collective-permute-done.15.b_ref = bf16[144,1024]{1,0:T(8,128)(2,1)S(1)} collective-permute-done((bf16[144,1024]{1,0:T(8,128)(2,1)S(1)}, bf16[144,1024]{1,0:T(8,128)(2,1)S(1)}, u32[]{:S(2)}, u32[]{:S(2)}) %collective-permute-start.15) | collective-permute-done | bytes 294944 | tf_op jit(solution)/shard_map/sums/ppermute | solution.py:44
  107.2 0.9 combine.1
  (23 shorter events, 2.7 us)
Async XLA Ops:
  0.8 14.3 %collective-permute-start.1 = (bf16[2,128,128]{2,1,0:T(8,128)(2,1)S(1)}, bf16[2,128,128]{2,1,0:T(8,128)(2,1)S(1)}, u32[]{:S(2)}, u32[]{:S(2)}) collective-permute-start(bf16[2,128,128]{2,1,0:T(8,128)(2,1)S(1)} %pad_maximum_fusion.1), channel_id=1, source_target_pairs={{0,128},{1,129},{2,130},{3,131},{4,132},{5,133},{6,134},{7,135},{8... | collective-permute-start | bytes 196616 | tf_op jit(solution)/shard_map/keys_x/ppermute | solution.py:44
  5.7 9.4 %collective-permute-start = (bf16[2,128,128]{2,1,0:T(8,128)(2,1)S(1)}, bf16[2,128,128]{2,1,0:T(8,128)(2,1)S(1)}, u32[]{:S(2)}, u32[]{:S(2)}) collective-permute-start(bf16[2,128,128]{2,1,0:T(8,128)(2,1)S(1)} %pad_maximum_fusion.1), channel_id=1, source_target_pairs={{0,0},{1,1},{2,2},{3,3},{4,4},{5,5},{6,6},{7,7},{8,72},{9,73},{10,... | collective-permute-start | bytes 196616 | tf_op jit(solution)/shard_map/keys_x/ppermute | solution.py:44
  8.3 11.4 %copy-start = (bf16[144,1024]{1,0:T(8,128)(2,1)S(1)}, bf16[144,1024]{1,0:T(8,128)(2,1)}, u32[]{:S(2)}) copy-start(bf16[144,1024]{1,0:T(8,128)(2,1)} %prep.1.refs_1_) | copy-start | bytes 884740
  15.2 15.6 %collective-permute-start.2 = (bf16[1,2,2,128,128]{4,3,2,1,0:T(8,128)(2,1)S(1)}, bf16[1,2,2,128,128]{4,3,2,1,0:T(8,128)(2,1)S(1)}, u32[]{:S(2)}, u32[]{:S(2)}) collective-permute-start(bf16[1,2,2,128,128]{4,3,2,1,0:T(8,128)(2,1)S(1)} %pair.1.refs_0_), channel_id=1, source_target_pairs={{0,4},{1,5},{2,6},{3,7},{4,0},{5,1},{6,2},{7,3},{8,12},{9,13},{10,... | collective-permute-start | bytes 393224 | tf_op jit(solution)/shard_map/keys_z1/ppermute | solution.py:44
  19.7 19.0 %collective-permute-start.5 = (bf16[144,1024]{1,0:T(8,128)(2,1)S(1)}, bf16[144,1024]{1,0:T(8,128)(2,1)S(1)}, u32[]{:S(2)}, u32[]{:S(2)}) collective-permute-start(bf16[144,1024]{1,0:T(8,128)(2,1)S(1)} %copy-done), channel_id=1, source_target_pairs={{0,1},{1,0},{2,3},{3,2},{4,5},{5,4},{6,7},{7,6},{8,9},{9,8},{10,11... | collective-permute-start | bytes 884744 | tf_op jit(solution)/shard_map/queries_z/ppermute | solution.py:44
  30.8 14.2 %collective-permute-start.3 = (bf16[2,2,2,128,128]{4,3,2,1,0:T(8,128)(2,1)S(1)}, bf16[2,2,2,128,128]{4,3,2,1,0:T(8,128)(2,1)S(1)}, u32[]{:S(2)}, u32[]{:S(2)}) collective-permute-start(bf16[2,2,2,128,128]{4,3,2,1,0:T(8,128)(2,1)S(1)} %join.5.refs_0_), channel_id=1, source_target_pairs={{0,2},{1,3},{2,0},{3,1},{4,6},{5,7},{6,4},{7,5},{8,10},{9,11},{10,... | collective-permute-start | bytes 786440 | tf_op jit(solution)/shard_map/keys_z2/ppermute | solution.py:44
  32.8 12.4 %collective-permute-start.4 = (bf16[2,2,2,128,128]{4,3,2,1,0:T(8,128)(2,1)S(1)}, bf16[2,2,2,128,128]{4,3,2,1,0:T(8,128)(2,1)S(1)}, u32[]{:S(2)}, u32[]{:S(2)}) collective-permute-start(bf16[2,2,2,128,128]{4,3,2,1,0:T(8,128)(2,1)S(1)} %join.5.refs_0_), channel_id=1, source_target_pairs={{0,8},{1,9},{2,10},{3,11},{4,12},{5,13},{6,14},{7,15},{8,0},{9,1},... | collective-permute-start | bytes 786440 | tf_op jit(solution)/shard_map/keys_y1/ppermute | solution.py:44
  39.6 14.6 %copy-start.1 = (s32[16]{0:T(128)S(1)}, s32[16]{0:T(128)}, u32[]{:S(2)}) copy-start(s32[16]{0:T(128)} %lengths.13) | copy-start | bytes 196
  39.6 14.6 %collective-permute-start.6 = (bf16[2,144,1024]{2,1,0:T(8,128)(2,1)}, bf16[2,144,1024]{2,1,0:T(8,128)(2,1)S(1)}, u32[]{:S(2)}, u32[]{:S(2)}) collective-permute-start(bf16[2,144,1024]{2,1,0:T(8,128)(2,1)} %pad_maximum_fusion), channel_id=1, source_target_pairs={{0,64},{1,65},{2,66},{3,67},{4,68},{5,69},{6,70},{7,71},{8,72},{9,... | collective-permute-start | bytes 1769480 | tf_op jit(solution)/shard_map/queries_x/ppermute | solution.py:44
  45.2 14.9 %collective-permute-start.8 = (bf16[4,2,2,128,128]{4,3,2,1,0:T(8,128)(2,1)S(1)}, bf16[4,2,2,128,128]{4,3,2,1,0:T(8,128)(2,1)S(1)}, u32[]{:S(2)}, u32[]{:S(2)}) collective-permute-start(bf16[4,2,2,128,128]{4,3,2,1,0:T(8,128)(2,1)S(1)} %join.7), channel_id=1, source_target_pairs={{0,24},{1,25},{2,26},{3,27},{4,28},{5,29},{6,30},{7,31},{8,16},{9,... | collective-permute-start | bytes 1572872 | tf_op jit(solution)/shard_map/keys_y2/ppermute | solution.py:44
  49.9 8.9 %collective-permute-start.7 = (bf16[2,2,2,128,128]{4,3,2,1,0:T(8,128)(2,1)S(1)}, bf16[2,2,2,128,128]{4,3,2,1,0:T(8,128)(2,1)S(1)}, u32[]{:S(2)}, u32[]{:S(2)}) collective-permute-start(bf16[2,2,2,128,128]{4,3,2,1,0:T(8,128)(2,1)S(1)} %collective-permute-done.3.refs_1_.refs_0_), channel_id=1, source_target_pairs={{0,8},{1,9},{2,10},{3,11},{4,12},{5,13},{6,14},{7,15},{8,0},{9,1},... | collective-permute-start | bytes 786440 | tf_op jit(solution)/shard_map/keys_y1/ppermute | solution.py:44
  52.2 19.9 %collective-permute-start.11 = (bf16[4,2,2,128,128]{4,3,2,1,0:T(8,128)(2,1)S(1)}, bf16[4,2,2,128,128]{4,3,2,1,0:T(8,128)(2,1)S(1)}, u32[]{:S(2)}, u32[]{:S(2)}) collective-permute-start(bf16[4,2,2,128,128]{4,3,2,1,0:T(8,128)(2,1)S(1)} %join.6.refs_0_), channel_id=1, source_target_pairs={{0,32},{1,33},{2,34},{3,35},{4,36},{5,37},{6,38},{7,39},{8,40},{9,... | collective-permute-start | bytes 1572872 | tf_op jit(solution)/shard_map/keys_c1/ppermute | solution.py:44
  60.1 11.9 %collective-permute-start.12 = (bf16[4,2,2,128,128]{4,3,2,1,0:T(8,128)(2,1)S(1)}, bf16[4,2,2,128,128]{4,3,2,1,0:T(8,128)(2,1)S(1)}, u32[]{:S(2)}, u32[]{:S(2)}) collective-permute-start(bf16[4,2,2,128,128]{4,3,2,1,0:T(8,128)(2,1)S(1)} %join.9.refs_0_), channel_id=1, source_target_pairs={{0,32},{1,33},{2,34},{3,35},{4,36},{5,37},{6,38},{7,39},{8,40},{9,... | collective-permute-start | bytes 1572872 | tf_op jit(solution)/shard_map/keys_c1/ppermute | solution.py:44
  62.1 14.9 %collective-permute-start.9 = (bf16[4,2,2,128,128]{4,3,2,1,0:T(8,128)(2,1)S(1)}, bf16[4,2,2,128,128]{4,3,2,1,0:T(8,128)(2,1)S(1)}, u32[]{:S(2)}, u32[]{:S(2)}) collective-permute-start(bf16[4,2,2,128,128]{4,3,2,1,0:T(8,128)(2,1)S(1)} %join.8), channel_id=1, source_target_pairs={{0,24},{1,25},{2,26},{3,27},{4,28},{5,29},{6,30},{7,31},{8,16},{9,... | collective-permute-start | bytes 1572872 | tf_op jit(solution)/shard_map/keys_y2/ppermute | solution.py:44
  66.5 10.5 %collective-permute-start.10 = (bf16[4,2,2,128,128]{4,3,2,1,0:T(8,128)(2,1)S(1)}, bf16[4,2,2,128,128]{4,3,2,1,0:T(8,128)(2,1)S(1)}, u32[]{:S(2)}, u32[]{:S(2)}) collective-permute-start(bf16[4,2,2,128,128]{4,3,2,1,0:T(8,128)(2,1)S(1)} %collective-permute-done.8.refs_0_), channel_id=1, source_target_pairs={{0,32},{1,33},{2,34},{3,35},{4,36},{5,37},{6,38},{7,39},{8,40},{9,... | collective-permute-start | bytes 1572872 | tf_op jit(solution)/shard_map/keys_c1/ppermute | solution.py:44
  77.0 7.1 %collective-permute-start.13 = (bf16[4,2,2,128,128]{4,3,2,1,0:T(8,128)(2,1)S(1)}, bf16[4,2,2,128,128]{4,3,2,1,0:T(8,128)(2,1)S(1)}, u32[]{:S(2)}, u32[]{:S(2)}) collective-permute-start(bf16[4,2,2,128,128]{4,3,2,1,0:T(8,128)(2,1)S(1)} %collective-permute-done.9.refs_1_), channel_id=1, source_target_pairs={{0,32},{1,33},{2,34},{3,35},{4,36},{5,37},{6,38},{7,39},{8,40},{9,... | collective-permute-start | bytes 1572872 | tf_op jit(solution)/shard_map/keys_c2/ppermute | solution.py:44
  86.1 14.6 %collective-permute-start.16 = (bf16[144,1024]{1,0:T(8,128)(2,1)S(1)}, bf16[144,1024]{1,0:T(8,128)(2,1)S(1)}, u32[]{:S(2)}, u32[]{:S(2)}) collective-permute-start(bf16[144,1024]{1,0:T(8,128)(2,1)S(1)} %last.2), channel_id=1, source_target_pairs={{0,65},{1,64},{2,67},{3,66},{4,69},{5,68},{6,71},{7,70},{8,73},{9,... | collective-permute-start | bytes 884744 | tf_op jit(solution)/shard_map/sums/ppermute | solution.py:44
  94.4 9.2 %collective-permute-start.14 = (bf16[144,1024]{1,0:T(8,128)(2,1)S(1)}, bf16[144,1024]{1,0:T(8,128)(2,1)S(1)}, u32[]{:S(2)}, u32[]{:S(2)}) collective-permute-start(bf16[144,1024]{1,0:T(8,128)(2,1)S(1)} %get-tuple-element.84), channel_id=1, source_target_pairs={{0,64},{1,65},{2,66},{3,67},{4,68},{5,69},{6,70},{7,71},{8,72},{9,... | collective-permute-start | bytes 884744 | tf_op jit(solution)/shard_map/sums/ppermute | solution.py:44
  98.6 8.6 %collective-permute-start.15 = (bf16[144,1024]{1,0:T(8,128)(2,1)S(1)}, bf16[144,1024]{1,0:T(8,128)(2,1)S(1)}, u32[]{:S(2)}, u32[]{:S(2)}) collective-permute-start(bf16[144,1024]{1,0:T(8,128)(2,1)S(1)} %get-tuple-element.85), channel_id=1, source_target_pairs={{0,1},{1,0},{2,3},{3,2},{4,5},{5,4},{6,7},{7,6},{8,9},{9,8},{10,11... | collective-permute-start | bytes 884744 | tf_op jit(solution)/shard_map/sums/ppermute | solution.py:44

commit v2 on v1

--- a/solution.py
+++ b/solution.py
@@ -264,21 +264,22 @@
 
 
 def final_kernel(kinds, n, cd, lengths, info, *refs):
-    tiles, (qt_ref, packed_ref, *state) = tiles_of(kinds, refs), refs[n : n + 5]
-    m_ref, l_ref, acc_ref = refs[n + 5 :]
+    tiles, (qt_ref, a_ref, b_ref, *state) = tiles_of(kinds, refs), refs[n : n + 6]
+    m_ref, l_ref, acc_ref = refs[n + 6 :]
     m_ref[0], l_ref[0], acc_ref[0] = (r[0] for r in state)
     fold(cd, lengths, info, tiles, 0, qt_ref, 0, m_ref, l_ref, acc_ref)
-    m_a, l_a, acc_a = unpacked(packed_ref)
-    m_b = m_ref[0]
-    top = jnp.maximum(m_a, m_b)
-    f_a, f_b = jnp.exp2(m_a - top), jnp.exp2(m_b - top)
-    m_ref[0] = top
-    l_ref[0] = l_a * f_a + l_ref[0] * f_b
-    acc_ref[0] = acc_a.astype(jnp.float32) * f_a + acc_ref[0] * f_b
-
-
-def combine_kernel(a_ref, b_ref, m_ref, l_ref, acc_ref, out_ref):
-    states = [unpacked(a_ref), unpacked(b_ref), (m_ref[0], l_ref[0], acc_ref[0])]
+    for packed_ref in (a_ref, b_ref):
+        m_a, l_a, acc_a = unpacked(packed_ref)
+        m_b = m_ref[0]
+        top = jnp.maximum(m_a, m_b)
+        f_a, f_b = jnp.exp2(m_a - top), jnp.exp2(m_b - top)
+        m_ref[0] = top
+        l_ref[0] = l_a * f_a + l_ref[0] * f_b
+        acc_ref[0] = acc_a.astype(jnp.float32) * f_a + acc_ref[0] * f_b
+
+
+def combine_kernel(a_ref, m_ref, l_ref, acc_ref, out_ref):
+    states = [unpacked(a_ref), (m_ref[0], l_ref[0], acc_ref[0])]
     top = functools.reduce(jnp.maximum, [m for m, _, _ in states])
     factors = [jnp.exp2(m - top) for m, _, _ in states]
     total = sum(f * l for f, (_, l, _) in zip(factors, states))
@@ -400,7 +401,7 @@
     kinds = [(1, ["two", "far"], 2)]
     far_o = [far_half_o, far_rest_o]
     sent = {}
-    for qis in ((3,), (2, 1)):
+    for qis in ((3,), (2,), (1,)):
         kernel = functools.partial(last_kernel, kinds, 2, qis)
         packed = call(
             kernel, "last", [PACKED] * len(qis), scalars, [*far_o, q4, *state], [VMEM] * len(qis), 1, SCRATCH
@@ -411,9 +412,9 @@
         got = {s: move(sent[s], to_slot(s)) for s in (3, 2, 1)}
     shape = [jax.ShapeDtypeStruct((1, *x.shape[1:]), x.dtype) for x in STATE]
     kernel = functools.partial(final_kernel, kinds, 2)
-    state = call(kernel, "final", shape, scalars, [*far_o, q4, got[3], *state], [VMEM] * 3, LONG)
+    state = call(kernel, "final", shape, scalars, [*far_o, q4, got[3], got[2], *state], [VMEM] * 3, LONG)
     out_shape = jax.ShapeDtypeStruct((TOKENS, ROWS), jnp.bfloat16)
-    return call(combine_kernel, "combine", out_shape, (), [got[2], got[1], *state], VMEM)
+    return call(combine_kernel, "combine", out_shape, (), [got[1], *state], VMEM)
 
 
 def solution(mesh):

time: 108 us -> 107 us (level)
  the two profiles are of different devices: /device:TPU:320 before, /device:TPU:354 now
where the time goes in v2:
time: 107 us; the launch traced here: 106 us
  starting transfers between devices  55.3 us (52%)
  waiting for transfers between devices  27.1 us (25%)
  Pallas kernels  21.5 us (20%)
  other arithmetic  1.67 us (2%)
    ppermute x17, starting transfers between devices, move(): return lax.ppermute(x, AXES, pairs)  55.3 us
    ppermute x17, waiting for transfers between devices, move(): return lax.ppermute(x, AXES, pairs)  27.1 us
    pallas_call x15, Pallas kernels, call(): pl.pallas_call(kernel, out_shape=out_shape, in_specs=[SMEM] * len(scalars...  19.6 us
  transfers between devices with their start and end apart: 17, of which 6 were waited for; matrix products, arithmetic and copies ran while one was open for 1% of the time, Pallas kernels for 16%

profile of v2, /device:TPU:354, one launch (start us, length us, event | category | flops | bytes accessed | tf_op | source)
XLA Modules:
  0.0 105.9 jit_solution(9681666639446431205)
XLA Ops:
  0.8 4.0 %collective-permute-start.1 = (bf16[2,128,128]{2,1,0:T(8,128)(2,1)S(1)}, bf16[2,128,128]{2,1,0:T(8,128)(2,1)S(1)}, u32[]{:S(2)}, u32[]{:S(2)}) collective-permute-start(bf16[2,128,128]{2,1,0:T(8,128)(2,1)S(1)} %pad_maximum_fusion.1), channel_id=1, source_target_pairs={{0,128},{1,129},{2,130},{3,131},{4,132},{5,133},{6,134},{7,135},{8... | collective-permute-start | bytes 196616 | tf_op jit(solution)/shard_map/keys_x/ppermute | solution.py:44
  5.5 1.9 %prep.1.refs_1_ = bf16[144,1024]{1,0:T(8,128)(2,1)} custom-call(bf16[128,1024]{1,0:T(8,128)(2,1)} %q_ref.1, bf16[128,128]{1,0:T(8,128)(2,1)} %k_ref.1), custom_call_target="tpu_custom_call" | custom-call | tf_op jit(solution)/shard_map/prep/pallas_call | solution.py:340
  7.4 8.9 %collective-permute-done.1.b_ref = bf16[2,128,128]{2,1,0:T(8,128)(2,1)S(1)} collective-permute-done((bf16[2,128,128]{2,1,0:T(8,128)(2,1)S(1)}, bf16[2,128,128]{2,1,0:T(8,128)(2,1)S(1)}, u32[]{:S(2)}, u32[]{:S(2)}) %collective-permute-start.1) | collective-permute-done | bytes 65568 | tf_op jit(solution)/shard_map/keys_x/ppermute | solution.py:44
  16.3 1.9 %collective-permute-start.2 = (bf16[1,2,2,128,128]{4,3,2,1,0:T(8,128)(2,1)S(1)}, bf16[1,2,2,128,128]{4,3,2,1,0:T(8,128)(2,1)S(1)}, u32[]{:S(2)}, u32[]{:S(2)}) collective-permute-start(bf16[1,2,2,128,128]{4,3,2,1,0:T(8,128)(2,1)S(1)} %pair.1.refs_0_), channel_id=1, source_target_pairs={{0,4},{1,5},{2,6},{3,7},{4,0},{5,1},{6,2},{7,3},{8,12},{9,13},{10,... | collective-permute-start | bytes 393224 | tf_op jit(solution)/shard_map/keys_z1/ppermute | solution.py:44
  18.2 4.4 %collective-permute-start.5 = (bf16[144,1024]{1,0:T(8,128)(2,1)S(1)}, bf16[144,1024]{1,0:T(8,128)(2,1)S(1)}, u32[]{:S(2)}, u32[]{:S(2)}) collective-permute-start(bf16[144,1024]{1,0:T(8,128)(2,1)S(1)} %copy-done), channel_id=1, source_target_pairs={{0,1},{1,0},{2,3},{3,2},{4,5},{5,4},{6,7},{7,6},{8,9},{9,8},{10,11... | collective-permute-start | bytes 884744 | tf_op jit(solution)/shard_map/queries_z/ppermute | solution.py:44
  22.7 5.8 %collective-permute-done.2.refs_1_ = bf16[1,2,2,128,128]{4,3,2,1,0:T(8,128)(2,1)S(1)} collective-permute-done((bf16[1,2,2,128,128]{4,3,2,1,0:T(8,128)(2,1)S(1)}, bf16[1,2,2,128,128]{4,3,2,1,0:T(8,128)(2,1)S(1)}, u32[]{:S(2)}, u32[]{:S(2)}) %collective-permute-start.2) | collective-permute-done | bytes 131104 | tf_op jit(solution)/shard_map/keys_z1/ppermute | solution.py:44
  28.5 11.1 %collective-permute-start.3 = (bf16[2,2,2,128,128]{4,3,2,1,0:T(8,128)(2,1)S(1)}, bf16[2,2,2,128,128]{4,3,2,1,0:T(8,128)(2,1)S(1)}, u32[]{:S(2)}, u32[]{:S(2)}) collective-permute-start(bf16[2,2,2,128,128]{4,3,2,1,0:T(8,128)(2,1)S(1)} %join.5.refs_0_), channel_id=1, source_target_pairs={{0,2},{1,3},{2,0},{3,1},{4,6},{5,7},{6,4},{7,5},{8,10},{9,11},{10,... | collective-permute-start | bytes 786440 | tf_op jit(solution)/shard_map/keys_z2/ppermute | solution.py:44
  39.5 2.0 %collective-permute-start.4 = (bf16[2,2,2,128,128]{4,3,2,1,0:T(8,128)(2,1)S(1)}, bf16[2,2,2,128,128]{4,3,2,1,0:T(8,128)(2,1)S(1)}, u32[]{:S(2)}, u32[]{:S(2)}) collective-permute-start(bf16[2,2,2,128,128]{4,3,2,1,0:T(8,128)(2,1)S(1)} %join.5.refs_0_), channel_id=1, source_target_pairs={{0,8},{1,9},{2,10},{3,11},{4,12},{5,13},{6,14},{7,15},{8,0},{9,1},... | collective-permute-start | bytes 786440 | tf_op jit(solution)/shard_map/keys_y1/ppermute | solution.py:44
  42.4 3.8 %collective-permute-start.6 = (bf16[2,144,1024]{2,1,0:T(8,128)(2,1)}, bf16[2,144,1024]{2,1,0:T(8,128)(2,1)S(1)}, u32[]{:S(2)}, u32[]{:S(2)}) collective-permute-start(bf16[2,144,1024]{2,1,0:T(8,128)(2,1)} %pad_maximum_fusion), channel_id=1, source_target_pairs={{0,64},{1,65},{2,66},{3,67},{4,68},{5,69},{6,70},{7,71},{8,72},{9,... | collective-permute-start | bytes 1769480 | tf_op jit(solution)/shard_map/queries_x/ppermute | solution.py:44
  46.2 4.3 %collective-permute-done.4.refs_1_.refs_0_ = bf16[2,2,2,128,128]{4,3,2,1,0:T(8,128)(2,1)S(1)} collective-permute-done((bf16[2,2,2,128,128]{4,3,2,1,0:T(8,128)(2,1)S(1)}, bf16[2,2,2,128,128]{4,3,2,1,0:T(8,128)(2,1)S(1)}, u32[]{:S(2)}, u32[]{:S(2)}) %collective-permute-start.4) | collective-permute-done | bytes 262176 | tf_op jit(solution)/shard_map/keys_y1/ppermute | solution.py:44
  50.5 3.2 %collective-permute-start.8 = (bf16[4,2,2,128,128]{4,3,2,1,0:T(8,128)(2,1)S(1)}, bf16[4,2,2,128,128]{4,3,2,1,0:T(8,128)(2,1)S(1)}, u32[]{:S(2)}, u32[]{:S(2)}) collective-permute-start(bf16[4,2,2,128,128]{4,3,2,1,0:T(8,128)(2,1)S(1)} %join.7), channel_id=1, source_target_pairs={{0,24},{1,25},{2,26},{3,27},{4,28},{5,29},{6,30},{7,31},{8,16},{9,... | collective-permute-start | bytes 1572872 | tf_op jit(solution)/shard_map/keys_y2/ppermute | solution.py:44
  53.7 3.8 %collective-permute-start.7 = (bf16[2,2,2,128,128]{4,3,2,1,0:T(8,128)(2,1)S(1)}, bf16[2,2,2,128,128]{4,3,2,1,0:T(8,128)(2,1)S(1)}, u32[]{:S(2)}, u32[]{:S(2)}) collective-permute-start(bf16[2,2,2,128,128]{4,3,2,1,0:T(8,128)(2,1)S(1)} %collective-permute-done.3.refs_1_.refs_0_), channel_id=1, source_target_pairs={{0,8},{1,9},{2,10},{3,11},{4,12},{5,13},{6,14},{7,15},{8,0},{9,1},... | collective-permute-start | bytes 786440 | tf_op jit(solution)/shard_map/keys_y1/ppermute | solution.py:44
  57.5 1.9 %collective-permute-start.11 = (bf16[4,2,2,128,128]{4,3,2,1,0:T(8,128)(2,1)S(1)}, bf16[4,2,2,128,128]{4,3,2,1,0:T(8,128)(2,1)S(1)}, u32[]{:S(2)}, u32[]{:S(2)}) collective-permute-start(bf16[4,2,2,128,128]{4,3,2,1,0:T(8,128)(2,1)S(1)} %join.6.refs_0_), channel_id=1, source_target_pairs={{0,32},{1,33},{2,34},{3,35},{4,36},{5,37},{6,38},{7,39},{8,40},{9,... | collective-permute-start | bytes 1572872 | tf_op jit(solution)/shard_map/keys_c1/ppermute | solution.py:44
  59.5 3.4 %own.1 = (s32[16]{0:T(128)S(1)}, bf16[4,144,1024]{2,1,0:T(8,128)(2,1)S(1)}, f32[4,1,1024]{2,1,0:T(1,128)S(1)}, f32[4,1,1024]{2,1,0:T(1,128)S(1)}, f32[4,128,1024]{2,1,0:T(8,128)S(1)}) custom-call(s32[1]{0:T(128)} %bitcast.cd, s32[16]{0:T(128)S(1)} %copy-done.1, bf16[4,2,2,128,128]{4,3,2,1,0:T(8,128)(2,1)S(1)} %join.6.refs_0_, bf16[144,1024]{1,0:T(8,128)(2,1)S(1)} %copy-done, ...), custom_call_target="tpu_custom_call" | custom-call | flops 1048576 | bytes 1024 | tf_op jit(solution)/shard_map/own/pallas_call | solution.py:310
  62.9 2.4 %collective-permute-start.12 = (bf16[4,2,2,128,128]{4,3,2,1,0:T(8,128)(2,1)S(1)}, bf16[4,2,2,128,128]{4,3,2,1,0:T(8,128)(2,1)S(1)}, u32[]{:S(2)}, u32[]{:S(2)}) collective-permute-start(bf16[4,2,2,128,128]{4,3,2,1,0:T(8,128)(2,1)S(1)} %join.9.refs_0_), channel_id=1, source_target_pairs={{0,32},{1,33},{2,34},{3,35},{4,36},{5,37},{6,38},{7,39},{8,40},{9,... | collective-permute-start | bytes 1572872 | tf_op jit(solution)/shard_map/keys_c1/ppermute | solution.py:44
  65.4 2.6 %collective-permute-start.9 = (bf16[4,2,2,128,128]{4,3,2,1,0:T(8,128)(2,1)S(1)}, bf16[4,2,2,128,128]{4,3,2,1,0:T(8,128)(2,1)S(1)}, u32[]{:S(2)}, u32[]{:S(2)}) collective-permute-start(bf16[4,2,2,128,128]{4,3,2,1,0:T(8,128)(2,1)S(1)} %join.8), channel_id=1, source_target_pairs={{0,24},{1,25},{2,26},{3,27},{4,28},{5,29},{6,30},{7,31},{8,16},{9,... | collective-permute-start | bytes 1572872 | tf_op jit(solution)/shard_map/keys_y2/ppermute | solution.py:44
  68.0 2.3 %collective-permute-start.10 = (bf16[4,2,2,128,128]{4,3,2,1,0:T(8,128)(2,1)S(1)}, bf16[4,2,2,128,128]{4,3,2,1,0:T(8,128)(2,1)S(1)}, u32[]{:S(2)}, u32[]{:S(2)}) collective-permute-start(bf16[4,2,2,128,128]{4,3,2,1,0:T(8,128)(2,1)S(1)} %collective-permute-done.8.refs_0_), channel_id=1, source_target_pairs={{0,32},{1,33},{2,34},{3,35},{4,36},{5,37},{6,38},{7,39},{8,40},{9,... | collective-permute-start | bytes 1572872 | tf_op jit(solution)/shard_map/keys_c1/ppermute | solution.py:44
  70.3 2.3 %one.1 = (f32[4,1,1024]{2,1,0:T(1,128)S(1)}, f32[4,1,1024]{2,1,0:T(1,128)S(1)}, f32[4,128,1024]{2,1,0:T(8,128)S(1)}) custom-call(s32[1]{0:T(128)} %bitcast.cd, s32[16]{0:T(128)S(1)} %copy-done.1, s32[16]{0:T(128)S(1)} %get-tuple-element.54.info, bf16[4,2,2,128,128]{4,3,2,1,0:T(8,128)(2,1)S(1)} %join.9.refs_0_, ...), custom_call_target="tpu_custom_call" | custom-call | flops 1048576 | bytes 1024 | tf_op jit(solution)/shard_map/one/pallas_call | solution.py:310
  72.6 3.8 %other.1 = (f32[4,1,1024]{2,1,0:T(1,128)S(1)}, f32[4,1,1024]{2,1,0:T(1,128)S(1)}, f32[4,128,1024]{2,1,0:T(8,128)S(1)}) custom-call(s32[1]{0:T(128)} %bitcast.cd, s32[16]{0:T(128)S(1)} %copy-done.1, s32[16]{0:T(128)S(1)} %get-tuple-element.54.info, bf16[4,2,2,128,128]{4,3,2,1,0:T(8,128)(2,1)S(1)} %collective-permute-done.11.refs_0_, ...), custom_call_target="tpu_custom_call" | custom-call | flops 1048576 | bytes 1024 | tf_op jit(solution)/shard_map/other/pallas_call | solution.py:310
  76.5 1.2 %collective-permute-done.9.refs_1_ = bf16[4,2,2,128,128]{4,3,2,1,0:T(8,128)(2,1)S(1)} collective-permute-done((bf16[4,2,2,128,128]{4,3,2,1,0:T(8,128)(2,1)S(1)}, bf16[4,2,2,128,128]{4,3,2,1,0:T(8,128)(2,1)S(1)}, u32[]{:S(2)}, u32[]{:S(2)}) %collective-permute-start.9) | collective-permute-done | bytes 524320 | tf_op jit(solution)/shard_map/keys_y2/ppermute | solution.py:44
  77.7 2.1 %collective-permute-start.13 = (bf16[4,2,2,128,128]{4,3,2,1,0:T(8,128)(2,1)S(1)}, bf16[4,2,2,128,128]{4,3,2,1,0:T(8,128)(2,1)S(1)}, u32[]{:S(2)}, u32[]{:S(2)}) collective-permute-start(bf16[4,2,2,128,128]{4,3,2,1,0:T(8,128)(2,1)S(1)} %collective-permute-done.9.refs_1_), channel_id=1, source_target_pairs={{0,32},{1,33},{2,34},{3,35},{4,36},{5,37},{6,38},{7,39},{8,40},{9,... | collective-permute-start | bytes 1572872 | tf_op jit(solution)/shard_map/keys_c2/ppermute | solution.py:44
  79.8 2.6 %far.1 = (f32[4,1,1024]{2,1,0:T(1,128)S(1)}, f32[4,1,1024]{2,1,0:T(1,128)S(1)}, f32[4,128,1024]{2,1,0:T(8,128)S(1)}) custom-call(s32[1]{0:T(128)} %bitcast.cd, s32[16]{0:T(128)S(1)} %copy-done.1, s32[16]{0:T(128)S(1)} %get-tuple-element.54.info, bf16[4,2,2,128,128]{4,3,2,1,0:T(8,128)(2,1)S(1)} %collective-permute-done.8.refs_0_, ...), custom_call_target="tpu_custom_call" | custom-call | flops 1048576 | bytes 1024 | tf_op jit(solution)/shard_map/far/pallas_call | solution.py:310
  82.4 1.4 %last.3 = bf16[144,1024]{1,0:T(8,128)(2,1)S(1)} custom-call(s32[1]{0:T(128)} %bitcast.cd, s32[16]{0:T(128)S(1)} %copy-done.1, s32[16]{0:T(128)S(1)} %get-tuple-element.54.info, bf16[4,2,2,128,128]{4,3,2,1,0:T(8,128)(2,1)S(1)} %collective-permute-done.10.refs_0_, bf16[4,2,2,128,128]{4,3,2,1,0:T(8,128)(2,1)S(1)} %collective-permute-done.13.refs_1_, ...), custom_call_target="tpu_custom_call" | custom-call | flops 1048576 | bytes 1024 | tf_op jit(solution)/shard_map/last/pallas_call | solution.py:310
  83.8 1.7 %last.4 = bf16[144,1024]{1,0:T(8,128)(2,1)S(1)} custom-call(s32[1]{0:T(128)} %bitcast.cd, s32[16]{0:T(128)S(1)} %copy-done.1, s32[16]{0:T(128)S(1)} %get-tuple-element.54.info, bf16[4,2,2,128,128]{4,3,2,1,0:T(8,128)(2,1)S(1)} %collective-permute-done.10.refs_0_, bf16[4,2,2,128,128]{4,3,2,1,0:T(8,128)(2,1)S(1)} %collective-permute-done.13.refs_1_, ...), custom_call_target="tpu_custom_call" | custom-call | flops 1048576 | bytes 1024 | tf_op jit(solution)/shard_map/last/pallas_call | solution.py:310
  85.5 2.5 %collective-permute-start.16 = (bf16[144,1024]{1,0:T(8,128)(2,1)S(1)}, bf16[144,1024]{1,0:T(8,128)(2,1)S(1)}, u32[]{:S(2)}, u32[]{:S(2)}) collective-permute-start(bf16[144,1024]{1,0:T(8,128)(2,1)S(1)} %last.4), channel_id=1, source_target_pairs={{0,64},{1,65},{2,66},{3,67},{4,68},{5,69},{6,70},{7,71},{8,72},{9,... | collective-permute-start | bytes 884744 | tf_op jit(solution)/shard_map/sums/ppermute | solution.py:44
  88.0 1.9 %collective-permute-start.15 = (bf16[144,1024]{1,0:T(8,128)(2,1)S(1)}, bf16[144,1024]{1,0:T(8,128)(2,1)S(1)}, u32[]{:S(2)}, u32[]{:S(2)}) collective-permute-start(bf16[144,1024]{1,0:T(8,128)(2,1)S(1)} %last.3), channel_id=1, source_target_pairs={{0,65},{1,64},{2,67},{3,66},{4,69},{5,68},{6,71},{7,70},{8,73},{9,... | collective-permute-start | bytes 884744 | tf_op jit(solution)/shard_map/sums/ppermute | solution.py:44
  89.9 1.4 %last.5 = bf16[144,1024]{1,0:T(8,128)(2,1)S(1)} custom-call(s32[1]{0:T(128)} %bitcast.cd, s32[16]{0:T(128)S(1)} %copy-done.1, s32[16]{0:T(128)S(1)} %get-tuple-element.54.info, bf16[4,2,2,128,128]{4,3,2,1,0:T(8,128)(2,1)S(1)} %collective-permute-done.10.refs_0_, bf16[4,2,2,128,128]{4,3,2,1,0:T(8,128)(2,1)S(1)} %collective-permute-done.13.refs_1_, ...), custom_call_target="tpu_custom_call" | custom-call | flops 1048576 | bytes 1024 | tf_op jit(solution)/shard_map/last/pallas_call | solution.py:310
  91.4 4.8 %collective-permute-start.14 = (bf16[144,1024]{1,0:T(8,128)(2,1)S(1)}, bf16[144,1024]{1,0:T(8,128)(2,1)S(1)}, u32[]{:S(2)}, u32[]{:S(2)}) collective-permute-start(bf16[144,1024]{1,0:T(8,128)(2,1)S(1)} %last.5), channel_id=1, source_target_pairs={{0,1},{1,0},{2,3},{3,2},{4,5},{5,4},{6,7},{7,6},{8,9},{9,8},{10,11... | collective-permute-start | bytes 884744 | tf_op jit(solution)/shard_map/sums/ppermute | solution.py:44
  96.2 5.7 %collective-permute-done.16.refs_4_ = bf16[144,1024]{1,0:T(8,128)(2,1)S(1)} collective-permute-done((bf16[144,1024]{1,0:T(8,128)(2,1)S(1)}, bf16[144,1024]{1,0:T(8,128)(2,1)S(1)}, u32[]{:S(2)}, u32[]{:S(2)}) %collective-permute-start.16) | collective-permute-done | bytes 294944 | tf_op jit(solution)/shard_map/sums/ppermute | solution.py:44
  101.9 1.9 %final.1 = (f32[1,1,1024]{2,1,0:T(1,128)S(1)}, f32[1,1,1024]{2,1,0:T(1,128)S(1)}, f32[1,128,1024]{2,1,0:T(8,128)S(1)}) custom-call(s32[1]{0:T(128)} %bitcast.cd, s32[16]{0:T(128)S(1)} %copy-done.1, s32[16]{0:T(128)S(1)} %get-tuple-element.54.info, bf16[4,2,2,128,128]{4,3,2,1,0:T(8,128)(2,1)S(1)} %collective-permute-done.10.refs_0_, ...), custom_call_target="tpu_custom_call" | custom-call | flops 8589934592 | bytes 8388608 | tf_op jit(solution)/shard_map/final/pallas_call | solution.py:310
  103.8 1.2 %collective-permute-done.14.a_ref = bf16[144,1024]{1,0:T(8,128)(2,1)S(1)} collective-permute-done((bf16[144,1024]{1,0:T(8,128)(2,1)S(1)}, bf16[144,1024]{1,0:T(8,128)(2,1)S(1)}, u32[]{:S(2)}, u32[]{:S(2)}) %collective-permute-start.14) | collective-permute-done | bytes 294944 | tf_op jit(solution)/shard_map/sums/ppermute | solution.py:44
  105.1 0.9 combine.1
  (24 shorter events, 2.6 us)
Async XLA Ops:
  0.8 15.4 %collective-permute-start.1 = (bf16[2,128,128]{2,1,0:T(8,128)(2,1)S(1)}, bf16[2,128,128]{2,1,0:T(8,128)(2,1)S(1)}, u32[]{:S(2)}, u32[]{:S(2)}) collective-permute-start(bf16[2,128,128]{2,1,0:T(8,128)(2,1)S(1)} %pad_maximum_fusion.1), channel_id=1, source_target_pairs={{0,128},{1,129},{2,130},{3,131},{4,132},{5,133},{6,134},{7,135},{8... | collective-permute-start | bytes 196616 | tf_op jit(solution)/shard_map/keys_x/ppermute | solution.py:44
  4.8 11.4 %collective-permute-start = (bf16[2,128,128]{2,1,0:T(8,128)(2,1)S(1)}, bf16[2,128,128]{2,1,0:T(8,128)(2,1)S(1)}, u32[]{:S(2)}, u32[]{:S(2)}) collective-permute-start(bf16[2,128,128]{2,1,0:T(8,128)(2,1)S(1)} %pad_maximum_fusion.1), channel_id=1, source_target_pairs={{0,0},{1,1},{2,2},{3,3},{4,4},{5,5},{6,6},{7,7},{8,72},{9,73},{10,... | collective-permute-start | bytes 196616 | tf_op jit(solution)/shard_map/keys_x/ppermute | solution.py:44
  7.4 10.9 %copy-start = (bf16[144,1024]{1,0:T(8,128)(2,1)S(1)}, bf16[144,1024]{1,0:T(8,128)(2,1)}, u32[]{:S(2)}) copy-start(bf16[144,1024]{1,0:T(8,128)(2,1)} %prep.1.refs_1_) | copy-start | bytes 884740
  16.3 12.2 %collective-permute-start.2 = (bf16[1,2,2,128,128]{4,3,2,1,0:T(8,128)(2,1)S(1)}, bf16[1,2,2,128,128]{4,3,2,1,0:T(8,128)(2,1)S(1)}, u32[]{:S(2)}, u32[]{:S(2)}) collective-permute-start(bf16[1,2,2,128,128]{4,3,2,1,0:T(8,128)(2,1)S(1)} %pair.1.refs_0_), channel_id=1, source_target_pairs={{0,4},{1,5},{2,6},{3,7},{4,0},{5,1},{6,2},{7,3},{8,12},{9,13},{10,... | collective-permute-start | bytes 393224 | tf_op jit(solution)/shard_map/keys_z1/ppermute | solution.py:44
  18.2 23.3 %collective-permute-start.5 = (bf16[144,1024]{1,0:T(8,128)(2,1)S(1)}, bf16[144,1024]{1,0:T(8,128)(2,1)S(1)}, u32[]{:S(2)}, u32[]{:S(2)}) collective-permute-start(bf16[144,1024]{1,0:T(8,128)(2,1)S(1)} %copy-done), channel_id=1, source_target_pairs={{0,1},{1,0},{2,3},{3,2},{4,5},{5,4},{6,7},{7,6},{8,9},{9,8},{10,11... | collective-permute-start | bytes 884744 | tf_op jit(solution)/shard_map/queries_z/ppermute | solution.py:44
  28.5 17.7 %collective-permute-start.3 = (bf16[2,2,2,128,128]{4,3,2,1,0:T(8,128)(2,1)S(1)}, bf16[2,2,2,128,128]{4,3,2,1,0:T(8,128)(2,1)S(1)}, u32[]{:S(2)}, u32[]{:S(2)}) collective-permute-start(bf16[2,2,2,128,128]{4,3,2,1,0:T(8,128)(2,1)S(1)} %join.5.refs_0_), channel_id=1, source_target_pairs={{0,2},{1,3},{2,0},{3,1},{4,6},{5,7},{6,4},{7,5},{8,10},{9,11},{10,... | collective-permute-start | bytes 786440 | tf_op jit(solution)/shard_map/keys_z2/ppermute | solution.py:44
  39.5 11.0 %collective-permute-start.4 = (bf16[2,2,2,128,128]{4,3,2,1,0:T(8,128)(2,1)S(1)}, bf16[2,2,2,128,128]{4,3,2,1,0:T(8,128)(2,1)S(1)}, u32[]{:S(2)}, u32[]{:S(2)}) collective-permute-start(bf16[2,2,2,128,128]{4,3,2,1,0:T(8,128)(2,1)S(1)} %join.5.refs_0_), channel_id=1, source_target_pairs={{0,8},{1,9},{2,10},{3,11},{4,12},{5,13},{6,14},{7,15},{8,0},{9,1},... | collective-permute-start | bytes 786440 | tf_op jit(solution)/shard_map/keys_y1/ppermute | solution.py:44
  42.4 17.1 %copy-start.1 = (s32[16]{0:T(128)S(1)}, s32[16]{0:T(128)}, u32[]{:S(2)}) copy-start(s32[16]{0:T(128)} %lengths.15) | copy-start | bytes 196
  42.4 17.1 %collective-permute-start.6 = (bf16[2,144,1024]{2,1,0:T(8,128)(2,1)}, bf16[2,144,1024]{2,1,0:T(8,128)(2,1)S(1)}, u32[]{:S(2)}, u32[]{:S(2)}) collective-permute-start(bf16[2,144,1024]{2,1,0:T(8,128)(2,1)} %pad_maximum_fusion), channel_id=1, source_target_pairs={{0,64},{1,65},{2,66},{3,67},{4,68},{5,69},{6,70},{7,71},{8,72},{9,... | collective-permute-start | bytes 1769480 | tf_op jit(solution)/shard_map/queries_x/ppermute | solution.py:44
  50.5 12.3 %collective-permute-start.8 = (bf16[4,2,2,128,128]{4,3,2,1,0:T(8,128)(2,1)S(1)}, bf16[4,2,2,128,128]{4,3,2,1,0:T(8,128)(2,1)S(1)}, u32[]{:S(2)}, u32[]{:S(2)}) collective-permute-start(bf16[4,2,2,128,128]{4,3,2,1,0:T(8,128)(2,1)S(1)} %join.7), channel_id=1, source_target_pairs={{0,24},{1,25},{2,26},{3,27},{4,28},{5,29},{6,30},{7,31},{8,16},{9,... | collective-permute-start | bytes 1572872 | tf_op jit(solution)/shard_map/keys_y2/ppermute | solution.py:44
  53.7 9.1 %collective-permute-start.7 = (bf16[2,2,2,128,128]{4,3,2,1,0:T(8,128)(2,1)S(1)}, bf16[2,2,2,128,128]{4,3,2,1,0:T(8,128)(2,1)S(1)}, u32[]{:S(2)}, u32[]{:S(2)}) collective-permute-start(bf16[2,2,2,128,128]{4,3,2,1,0:T(8,128)(2,1)S(1)} %collective-permute-done.3.refs_1_.refs_0_), channel_id=1, source_target_pairs={{0,8},{1,9},{2,10},{3,11},{4,12},{5,13},{6,14},{7,15},{8,0},{9,1},... | collective-permute-start | bytes 786440 | tf_op jit(solution)/shard_map/keys_y1/ppermute | solution.py:44
  57.5 15.1 %collective-permute-start.11 = (bf16[4,2,2,128,128]{4,3,2,1,0:T(8,128)(2,1)S(1)}, bf16[4,2,2,128,128]{4,3,2,1,0:T(8,128)(2,1)S(1)}, u32[]{:S(2)}, u32[]{:S(2)}) collective-permute-start(bf16[4,2,2,128,128]{4,3,2,1,0:T(8,128)(2,1)S(1)} %join.6.refs_0_), channel_id=1, source_target_pairs={{0,32},{1,33},{2,34},{3,35},{4,36},{5,37},{6,38},{7,39},{8,40},{9,... | collective-permute-start | bytes 1572872 | tf_op jit(solution)/shard_map/keys_c1/ppermute | solution.py:44
  62.9 9.7 %collective-permute-start.12 = (bf16[4,2,2,128,128]{4,3,2,1,0:T(8,128)(2,1)S(1)}, bf16[4,2,2,128,128]{4,3,2,1,0:T(8,128)(2,1)S(1)}, u32[]{:S(2)}, u32[]{:S(2)}) collective-permute-start(bf16[4,2,2,128,128]{4,3,2,1,0:T(8,128)(2,1)S(1)} %join.9.refs_0_), channel_id=1, source_target_pairs={{0,32},{1,33},{2,34},{3,35},{4,36},{5,37},{6,38},{7,39},{8,40},{9,... | collective-permute-start | bytes 1572872 | tf_op jit(solution)/shard_map/keys_c1/ppermute | solution.py:44
  65.4 12.3 %collective-permute-start.9 = (bf16[4,2,2,128,128]{4,3,2,1,0:T(8,128)(2,1)S(1)}, bf16[4,2,2,128,128]{4,3,2,1,0:T(8,128)(2,1)S(1)}, u32[]{:S(2)}, u32[]{:S(2)}) collective-permute-start(bf16[4,2,2,128,128]{4,3,2,1,0:T(8,128)(2,1)S(1)} %join.8), channel_id=1, source_target_pairs={{0,24},{1,25},{2,26},{3,27},{4,28},{5,29},{6,30},{7,31},{8,16},{9,... | collective-permute-start | bytes 1572872 | tf_op jit(solution)/shard_map/keys_y2/ppermute | solution.py:44
  68.0 9.7 %collective-permute-start.10 = (bf16[4,2,2,128,128]{4,3,2,1,0:T(8,128)(2,1)S(1)}, bf16[4,2,2,128,128]{4,3,2,1,0:T(8,128)(2,1)S(1)}, u32[]{:S(2)}, u32[]{:S(2)}) collective-permute-start(bf16[4,2,2,128,128]{4,3,2,1,0:T(8,128)(2,1)S(1)} %collective-permute-done.8.refs_0_), channel_id=1, source_target_pairs={{0,32},{1,33},{2,34},{3,35},{4,36},{5,37},{6,38},{7,39},{8,40},{9,... | collective-permute-start | bytes 1572872 | tf_op jit(solution)/shard_map/keys_c1/ppermute | solution.py:44
  77.7 4.7 %collective-permute-start.13 = (bf16[4,2,2,128,128]{4,3,2,1,0:T(8,128)(2,1)S(1)}, bf16[4,2,2,128,128]{4,3,2,1,0:T(8,128)(2,1)S(1)}, u32[]{:S(2)}, u32[]{:S(2)}) collective-permute-start(bf16[4,2,2,128,128]{4,3,2,1,0:T(8,128)(2,1)S(1)} %collective-permute-done.9.refs_1_), channel_id=1, source_target_pairs={{0,32},{1,33},{2,34},{3,35},{4,36},{5,37},{6,38},{7,39},{8,40},{9,... | collective-permute-start | bytes 1572872 | tf_op jit(solution)/shard_map/keys_c2/ppermute | solution.py:44
  85.5 16.4 %collective-permute-start.16 = (bf16[144,1024]{1,0:T(8,128)(2,1)S(1)}, bf16[144,1024]{1,0:T(8,128)(2,1)S(1)}, u32[]{:S(2)}, u32[]{:S(2)}) collective-permute-start(bf16[144,1024]{1,0:T(8,128)(2,1)S(1)} %last.4), channel_id=1, source_target_pairs={{0,64},{1,65},{2,66},{3,67},{4,68},{5,69},{6,70},{7,71},{8,72},{9,... | collective-permute-start | bytes 884744 | tf_op jit(solution)/shard_map/sums/ppermute | solution.py:44
  88.0 13.9 %collective-permute-start.15 = (bf16[144,1024]{1,0:T(8,128)(2,1)S(1)}, bf16[144,1024]{1,0:T(8,128)(2,1)S(1)}, u32[]{:S(2)}, u32[]{:S(2)}) collective-permute-start(bf16[144,1024]{1,0:T(8,128)(2,1)S(1)} %last.3), channel_id=1, source_target_pairs={{0,65},{1,64},{2,67},{3,66},{4,69},{5,68},{6,71},{7,70},{8,73},{9,... | collective-permute-start | bytes 884744 | tf_op jit(solution)/shard_map/sums/ppermute | solution.py:44
  91.4 13.7 %collective-permute-start.14 = (bf16[144,1024]{1,0:T(8,128)(2,1)S(1)}, bf16[144,1024]{1,0:T(8,128)(2,1)S(1)}, u32[]{:S(2)}, u32[]{:S(2)}) collective-permute-start(bf16[144,1024]{1,0:T(8,128)(2,1)S(1)} %last.5), channel_id=1, source_target_pairs={{0,1},{1,0},{2,3},{3,2},{4,5},{5,4},{6,7},{7,6},{8,9},{9,8},{10,11... | collective-permute-start | bytes 884744 | tf_op jit(solution)/shard_map/sums/ppermute | solution.py:44
